TPU v7x, 32 devices: a whole 2x2x4 slice. The times are simulated.
32 devices in a mesh: dp: 32 (over z, y, x, core).
Axes of the slice: x: 2, y: 2, z: 4, core: 2. Of those that a mesh axis runs over, the one named last changes fastest.
Arguments:
- tokens: bfloat16 [32768, 768], P('dp'), may hold values from -6 to 6
- lengths: int32 [64], P('dp'), may hold values from 65 to 512, as said below
- partners: int32 [64], replicated, may hold values from 0 to 63, each once
- targets: float32 [64], P('dp'), may hold values from 0 to 1
- query_proj: bfloat16 [768, 768], replicated, may hold values from -0.21875 to 0.21875
- query_bias: float32 [768], replicated, may hold values from -0.6 to 0.6
- key_proj: bfloat16 [768, 768], replicated, may hold values from -0.21875 to 0.21875
- value_proj: bfloat16 [768, 768], replicated, may hold values from -0.21875 to 0.21875
- value_bias: float32 [768], replicated, may hold values from -0.6 to 0.6
- mixer_proj: bfloat16 [768, 768], replicated, may hold values from -0.875 to 0.875
- mixer_bias: float32 [768], replicated, may hold values from -0.3 to 0.3
- first_gain: float32 [768], replicated, may hold values from 0.5 to 1.5
- first_shift: float32 [768], replicated, may hold values from -0.3 to 0.3
- expand_proj: bfloat16 [768, 3072], replicated, may hold values from -0.21875 to 0.21875
- expand_bias: float32 [3072], replicated, may hold values from -0.6 to 0.6
- shrink_proj: bfloat16 [3072, 768], replicated, may hold values from -0.109375 to 0.109375
- shrink_bias: float32 [768], replicated, may hold values from -0.3 to 0.3
- second_gain: float32 [768], replicated, may hold values from 0.5 to 1.5
- second_shift: float32 [768], replicated, may hold values from -0.3 to 0.3
Outputs:
- pair_scores: float32 [64], P('dp')
- tokens_grad: float32 [32768, 768], P('dp')
- query_proj_grad: float32 [768, 768], replicated
- query_bias_grad: float32 [768], replicated
- key_proj_grad: float32 [768, 768], replicated
- value_proj_grad: float32 [768, 768], replicated
- value_bias_grad: float32 [768], replicated
- mixer_proj_grad: float32 [768, 768], replicated
- mixer_bias_grad: float32 [768], replicated
- first_gain_grad: float32 [768], replicated
- first_shift_grad: float32 [768], replicated
- expand_proj_grad: float32 [768, 3072], replicated
- expand_bias_grad: float32 [3072], replicated
- shrink_proj_grad: float32 [3072, 768], replicated
- shrink_bias_grad: float32 [768], replicated
- second_gain_grad: float32 [768], replicated
- second_shift_grad: float32 [768], replicated
Inputs may be any that keep to these rules, and one draw needn't show every extreme that they name: `lengths`: the 2 sentences of one device share one bucket with most 128, 256 or 512, and each length is above half of its bucket's most; some sentence is exactly 512 long. `partners`: every sentence is the partner of exactly one sentence.
All inputs are finite; a program needn't handle non-finite values.
Results may differ from a plain program's by a relative error of at most 0.012.
Values sent between devices are 32-bit elements; how exact they have to be, the bound alone decides.
A program may use at most 192 MiB of HBM per device.

v0:
```python
from functools import partial
import math

import jax
import jax.numpy as jnp
from jax import lax
from jax.sharding import PartitionSpec as P

H = 12


def to_low(value):
    return value.astype(jnp.bfloat16)


def tdot(left, right):
    return lax.dot_general(
        left, right, (((0,), (0,)), ((), ())), preferred_element_type=jnp.float32
    )


def ndot(left, right):
    return lax.dot_general(
        left, right, (((1,), (1,)), ((), ())), preferred_element_type=jnp.float32
    )


def norm_rows(rows, gain, shift):
    mean = jnp.mean(rows, axis=-1, keepdims=True)
    centred = rows - mean
    spread = jnp.mean(centred * centred, axis=-1, keepdims=True)
    inverse = lax.rsqrt(spread + 1e-06)
    normed = centred * inverse
    return (normed * gain + shift, normed, inverse)


def norm_back(upstream, normed, inverse, gain):
    gain_grad = jnp.sum(upstream * normed, axis=0)
    shift_grad = jnp.sum(upstream, axis=0)
    dnormed = upstream * gain
    first_mean = jnp.mean(dnormed, axis=-1, keepdims=True)
    second_mean = jnp.mean(dnormed * normed, axis=-1, keepdims=True)
    return (inverse * (dnormed - first_mean - normed * second_mean), gain_grad, shift_grad)


def per_device(
    tokens,
    lengths,
    partners,
    targets,
    query_proj,
    query_bias,
    key_proj,
    value_proj,
    value_bias,
    mixer_proj,
    mixer_bias,
    first_gain,
    first_shift,
    expand_proj,
    expand_bias,
    shrink_proj,
    shrink_bias,
    second_gain,
    second_shift,
):
    sents = lengths.shape[0]
    rows_all = tokens.shape[0]
    slot = rows_all // sents
    width = tokens.shape[1]
    heads = H
    depth = width // heads
    scale = 1.0 / math.sqrt(depth)
    total = partners.shape[0]
    base = lax.axis_index("dp") * sents
    highest = lax.Precision.HIGHEST
    places = jnp.arange(slot, dtype=jnp.int32)
    valid = places[None, :] < lengths[:, None]
    row_mask = valid.reshape(rows_all, 1).astype(jnp.float32)
    shape4 = (sents, slot, heads, depth)
    queries = to_low(jnp.dot(tokens, query_proj, preferred_element_type=jnp.float32) + query_bias)
    keys = to_low(jnp.dot(tokens, key_proj, preferred_element_type=jnp.float32))
    values = to_low(jnp.dot(tokens, value_proj, preferred_element_type=jnp.float32) + value_bias)
    queries4 = queries.reshape(shape4)
    keys4 = keys.reshape(shape4)
    values4 = values.reshape(shape4)

    def masked_scores(query_rows, key_rows, live):
        raw = (
            jnp.einsum("qhd,khd->hqk", query_rows, key_rows, preferred_element_type=jnp.float32)
            * scale
        )
        return jnp.where(live[None, None, :], raw, -1000000000.0)

    def attend(item):
        query_rows, key_rows, value_rows, live = item
        raw = masked_scores(query_rows, key_rows, live)
        top = jnp.max(raw, axis=-1, keepdims=True)
        expd = jnp.exp(raw - top)
        summed = jnp.sum(expd, axis=-1, keepdims=True)
        probs = to_low(expd / summed)
        mixed = jnp.einsum("hqk,khd->qhd", probs, value_rows, preferred_element_type=jnp.float32)
        return (mixed, (top + jnp.log(summed))[..., 0])

    mixed, logsum = lax.map(attend, (queries4, keys4, values4, valid))
    mixed_low = to_low(mixed.reshape(rows_all, width))
    branch = jnp.dot(mixed_low, mixer_proj, preferred_element_type=jnp.float32) + mixer_bias
    first_out, first_normed, first_inverse = norm_rows(
        tokens.astype(jnp.float32) + branch, first_gain, first_shift
    )
    first_low = to_low(first_out)
    pre = jnp.dot(first_low, expand_proj, preferred_element_type=jnp.float32) + expand_bias
    act, gelu_back = jax.vjp(partial(jax.nn.gelu, approximate=False), pre)
    act_low = to_low(act)
    shrink = jnp.dot(act_low, shrink_proj, preferred_element_type=jnp.float32) + shrink_bias
    outputs, second_normed, second_inverse = norm_rows(
        first_out + shrink, second_gain, second_shift
    )
    counts = lengths.astype(jnp.float32)
    pooled = jnp.sum((outputs * row_mask).reshape(sents, slot, width), axis=1) / counts[:, None]
    mine = lax.dynamic_slice_in_dim(partners, base, sents)
    every = lax.all_gather(pooled, "dp", axis=0, tiled=True)
    partner_vec = jnp.take(every, mine, axis=0)
    inner = jnp.sum(pooled * partner_vec, axis=-1)
    own_len = jnp.sqrt(jnp.sum(pooled * pooled, axis=-1) + 1e-06)
    far_len = jnp.sqrt(jnp.sum(partner_vec * partner_vec, axis=-1) + 1e-06)
    pair_scores = inner / (own_len * far_len)
    miss = pair_scores - targets
    joint = (own_len * far_len)[:, None]
    dpooled = miss[:, None] * (
        partner_vec / joint - (pair_scores / (own_len * own_len))[:, None] * pooled
    )
    dpartner = miss[:, None] * (
        pooled / joint - (pair_scores / (far_len * far_len))[:, None] * partner_vec
    )
    owners = (mine[:, None] == jnp.arange(total, dtype=jnp.int32)[None, :]).astype(jnp.float32)
    spread = lax.dot_general(owners, dpartner, (((0,), (0,)), ((), ())), precision=highest)
    returned = lax.psum_scatter(spread, "dp", scatter_dimension=0, tiled=True)
    dpool_all = (dpooled + returned) / counts[:, None]
    doutputs = (dpool_all[:, None, :] * valid[:, :, None].astype(jnp.float32)).reshape(
        rows_all, width
    )
    dsecond, second_gain_grad, second_shift_grad = norm_back(
        doutputs, second_normed, second_inverse, second_gain
    )
    dshrink = to_low(dsecond)
    shrink_proj_grad = tdot(act_low, dshrink)
    shrink_bias_grad = jnp.sum(dshrink.astype(jnp.float32), axis=0)
    dact = ndot(dshrink, shrink_proj)
    dpre = to_low(gelu_back(dact)[0])
    expand_proj_grad = tdot(first_low, dpre)
    expand_bias_grad = jnp.sum(dpre.astype(jnp.float32), axis=0)
    dfirst_out = ndot(dpre, expand_proj) + dsecond
    dfirst, first_gain_grad, first_shift_grad = norm_back(
        dfirst_out, first_normed, first_inverse, first_gain
    )
    dbranch = to_low(dfirst)
    mixer_proj_grad = tdot(mixed_low, dbranch)
    mixer_bias_grad = jnp.sum(dbranch.astype(jnp.float32), axis=0)
    dmixed = to_low(ndot(dbranch, mixer_proj)).reshape(shape4)

    def attend_back(item):
        query_rows, key_rows, value_rows, live, row_logsum, dmix = item
        raw = masked_scores(query_rows, key_rows, live)
        probs = jnp.exp(raw - row_logsum[..., None])
        probs_low = to_low(probs)
        dprob = jnp.einsum("qhd,khd->hqk", dmix, value_rows, preferred_element_type=jnp.float32)
        delta = jnp.sum(dprob * probs, axis=-1, keepdims=True)
        dscore = to_low(probs * (dprob - delta))
        dquery = (
            jnp.einsum("hqk,khd->qhd", dscore, key_rows, preferred_element_type=jnp.float32) * scale
        )
        dkey = (
            jnp.einsum("hqk,qhd->khd", dscore, query_rows, preferred_element_type=jnp.float32)
            * scale
        )
        dvalue = jnp.einsum("hqk,qhd->khd", probs_low, dmix, preferred_element_type=jnp.float32)
        return (to_low(dquery), to_low(dkey), to_low(dvalue))

    dquery, dkey, dvalue = lax.map(attend_back, (queries4, keys4, values4, valid, logsum, dmixed))
    dquery = dquery.reshape(rows_all, width)
    dkey = dkey.reshape(rows_all, width)
    dvalue = dvalue.reshape(rows_all, width)
    query_proj_grad = tdot(tokens, dquery)
    query_bias_grad = jnp.sum(dquery.astype(jnp.float32), axis=0)
    key_proj_grad = tdot(tokens, dkey)
    value_proj_grad = tdot(tokens, dvalue)
    value_bias_grad = jnp.sum(dvalue.astype(jnp.float32), axis=0)
    tokens_grad = (
        ndot(dquery, query_proj) + ndot(dkey, key_proj) + ndot(dvalue, value_proj) + dfirst
    )
    (
        query_proj_grad,
        query_bias_grad,
        key_proj_grad,
        value_proj_grad,
        value_bias_grad,
        mixer_proj_grad,
        mixer_bias_grad,
        first_gain_grad,
        first_shift_grad,
        expand_proj_grad,
        expand_bias_grad,
        shrink_proj_grad,
        shrink_bias_grad,
        second_gain_grad,
        second_shift_grad,
    ) = lax.psum(
        (
            query_proj_grad,
            query_bias_grad,
            key_proj_grad,
            value_proj_grad,
            value_bias_grad,
            mixer_proj_grad,
            mixer_bias_grad,
            first_gain_grad,
            first_shift_grad,
            expand_proj_grad,
            expand_bias_grad,
            shrink_proj_grad,
            shrink_bias_grad,
            second_gain_grad,
            second_shift_grad,
        ),
        "dp",
    )
    return (
        pair_scores,
        tokens_grad,
        query_proj_grad,
        query_bias_grad,
        key_proj_grad,
        value_proj_grad,
        value_bias_grad,
        mixer_proj_grad,
        mixer_bias_grad,
        first_gain_grad,
        first_shift_grad,
        expand_proj_grad,
        expand_bias_grad,
        shrink_proj_grad,
        shrink_bias_grad,
        second_gain_grad,
        second_shift_grad,
    )


def solution(mesh):
    in_specs = (
        P("dp", None),
        P("dp"),
        P(),
        P("dp"),
        P(),
        P(),
        P(),
        P(),
        P(),
        P(),
        P(),
        P(),
        P(),
        P(),
        P(),
        P(),
        P(),
        P(),
        P(),
    )
    out_specs = (
        P("dp"),
        P("dp", None),
        P(),
        P(),
        P(),
        P(),
        P(),
        P(),
        P(),
        P(),
        P(),
        P(),
        P(),
        P(),
        P(),
        P(),
        P(),
    )
    return jax.shard_map(
        per_device, mesh=mesh, in_specs=in_specs, out_specs=out_specs, check_vma=False
    )
```

profile of v0, /device:TPU:0, one launch (start us, length us, event | category | flops | bytes accessed | tf_op | source)
XLA Modules:
  0.0 889.9 jit_solution(847159666619956149)
XLA Ops:
  9.8 4.3 add_convert_fusion.2
  35.2 3.8 reshape.244
  42.0 21.9 %while.26 = (s32[]{:T(128)}, bf16[2,512,12,64]{1,3,2,0:T(8,128)(2,1)}, f32[2,12,512]{2,1,0:T(8,128)S(1)}, bf16[2,512,12,64]{1,3,2,0:T(8,128)(2,1)}, pred[2,512]{...) while((s32[]{:T(128)}, ...), condition=%wide.region_3.4_spmd, body=%wide.region_0.3_spmd.sunk | while | flops 843048960 | bytes 48214648 | solution.py:105
  42.2 4.1 fusion.149
  48.9 4.2 bitcast_dynamic-update-slice_fusion.4
  53.1 4.0 fusion.149
  59.8 4.2 bitcast_dynamic-update-slice_fusion.4
  72.5 35.2 %multiply_convert_fusion.3 = (bf16[1024,3072]{1,0:T(8,128)(2,1)S(1)}, f32[1024,3072]{1,0:T(8,128)}, f32[1024,3072]{1,0:T(8,128)}) fusion(f32[3072]{0:T(1024)S(1)} %copy-done.60, bf16[768,3072]{1,0:T(8,128)(2,1)S(1)} %bitcast.217, f32[1024,768]{1,0:T(8,128)S(1)} %get-tuple-element.299, f32[768]{0:T(1024)S(1)} %copy-done.38, f32[768]{0:T(1024)S(1)} %copy-done.36, ...), kind=kOutput, calls=%fused_computation.65 | convolution fusion | flops 5043388416 | bytes 39348224 | tf_op jit(solution)/shard_map/dot_general | solution.py:112
  107.7 5.5 fusion.94
  115.0 43.7 %all-gather = f32[32,2,768]{2,1,0:T(2,128)S(1)} all-gather(f32[1,2,768]{2,1,0:T(2,128)S(1)} %fusion.132), channel_id=1, replica_groups=mesh['dp'=32] {'dp'}, dimensions={0}, use_global_device_ids=true | all-gather | bytes 202752 | tf_op jit(solution)/shard_map/all_gather | solution.py:122
  161.5 119.2 %all-reduce.6.cloned.1.call-done = f32[64,768]{1,0:T(8,128)} async-done(((f32[64,768]{1,0:T(8,128)}), f32[64,768]{1,0:T(8,128)}) %all-reduce.6.cloned.1.call-update) | async-done | bytes 196624
  289.7 10.1 %fusion.97 = f32[3072,768]{1,0:T(8,128)} fusion(bf16[1024,3072]{1,0:T(8,128)(2,1)} %copy-done.64, bf16[1024,768]{1,0:T(8,128)(2,1)S(1)} %get-tuple-element.277), kind=kOutput, calls=%fused_computation.166 | convolution fusion | flops 4831838208 | bytes 17301504 | tf_op jit(solution)/shard_map/dot_general | solution.py:17
  299.8 17.5 %convert_reduce_fusion = (f32[3072]{0:T(1024)}, bf16[1024,3072]{1,0:T(8,128)(2,1)}) fusion(f32[1024,3072]{1,0:T(8,128)} %get-tuple-element.287, bf16[1024,768]{1,0:T(8,128)(2,1)S(1)} %get-tuple-element.277, bf16[3072,768]{1,0:T(8,128)(2,1)} %param.38, f32[1024,3072]{1,0:T(8,128)} %get-tuple-element.300, f32[3072]{0:T(1024)S(1)} %copy-done.60), kind=kOutput, calls=%fused_computation.63 | convolution fusion | flops 4885312512 | bytes 37773312 | tf_op jit(solution)/shard_map/dot_general | solution.py:23
  317.3 11.0 %fusion.85 = f32[768,3072]{1,0:T(8,128)} fusion(bf16[1024,3072]{1,0:T(8,128)(2,1)} %get-tuple-element.305, f32[1024,768]{1,0:T(8,128)S(1)} %copy-done.8, f32[768]{0:T(1024)S(1)} %copy-done.38, f32[768]{0:T(1024)S(1)} %copy-done.36, f32[1024]{0:T(1024)S(1)} %add_rsqrt_fusion.1, f32[1024]{0:T(1024)S(1)} %broadcast_multiply_fusion.4), kind=kOutput, calls=%fused_computation.159 | convolution fusion | flops 4835770368 | bytes 18888704 | tf_op jit(solution)/shard_map/dot_general | solution.py:17
  328.3 9.1 %multiply_reduce_fusion.2 = (f32[768]{0:T(1024)}, f32[1024]{0:T(1024)S(1)}, f32[1024]{0:T(1024)S(1)}, f32[768]{0:T(1024)}, f32[1024,768]{1,0:T(8,128)S(1)}) fusion(f32[1024,768]{1,0:T(8,128)S(1)} %copy-done.8, f32[1024]{0:T(1024)S(1)} %add_rsqrt_fusion.1, f32[1024]{0:T(1024)S(1)} %broadcast_multiply_fusion.4, f32[768]{0:T(1024)S(1)} %copy-done.36, ...), kind=kOutput, calls=%fused_computation.93 | convolution fusion | flops 4839698432 | bytes 20472832 | tf_op jit(solution)/shard_map/dot_general | solution.py:23
  346.1 4.0 reshape.246
  353.0 52.2 %while.27 = (s32[]{:T(128)}, bf16[2,512,12,64]{1,3,2,0:T(8,128)(2,1)}, bf16[2,512,12,64]{1,3,2,0:T(8,128)(2,1)}, bf16[2,512,12,64]{1,3,2,0:T(8,128)(2,1)}, bf16[...) while((s32[]{:T(128)}, ...), condition=%wide.region_19.20_spmd, body=%wide.region_17.19_spmd.sunk | while | flops 2062411776 | bytes 146472784 | solution.py:180
  356.4 7.3 multiply_reduce_fusion.11
  363.7 7.2 multiply_convert_fusion.5
  382.3 7.3 multiply_reduce_fusion.11
  389.6 7.2 multiply_convert_fusion.5
  424.7 44.9 %all-reduce.1 = (f32[768]{0:T(1024)}, f32[768]{0:T(1024)}, f32[768]{0:T(1024)}, f32[768]{0:T(1024)}, f32[768]{0:T(1024)}, /*index=5*/f32[3072]{0:T(1024)}, f32[768]{0:T(1024)}, f32[768]{0:T(1024)}, f32[768]{0:T(1024)}) all-reduce(f32[768]{0:T(1024)S(1)} %reduce_sum.224, f32[768]{0:T(1024)S(1)} %reduce_sum.226, ...), channel_id=1, replica_groups=mesh['dp'=32] {'dp'}, use_global_device_ids=true, to_apply=%region_22.23 | all-reduce | flops 9216 | bytes 73728 | tf_op jit(solution)/shard_map/psum | solution.py:208
  479.6 380.1 %all-reduce.8.cloned.1.call-done = (f32[768,768]{0,1:T(8,128)}, f32[768,768]{0,1:T(8,128)}, f32[768,768]{0,1:T(8,128)}, f32[768,768]{1,0:T(8,128)}, f32[768,3072]{1,0:T(8,128)}, /*index=5*/f32[3072,768]{1,0:T(8,128)}) async-done(((f32[768,768]{0,1:T(8,128)}, f32[768,768]{0,1:T(8,128)}, f32[768,768]{0,1:T(8,128)}, f32[768,768]{1,0:T(8,128)}, f32[768,3072]{1,0:T(8,128)}, /*index=5*/f32[3072,768]{1,0:T(8,128)}), ...) | async-done | bytes 28311568 | tf_op jit(solution)/shard_map/psum | solution.py:208
  869.5 9.3 %copy.140 = f32[768,3072]{1,0:T(8,128)} copy(f32[768,3072]{1,0:T(8,128)} %get-tuple-element.488) | data formatting | bytes 18874368
  (257 shorter events, 130.5 us)
Async XLA Ops:
  7.2 60.9 %copy-start = (bf16[768,768]{1,0:T(8,128)(2,1)S(1)}, bf16[768,768]{1,0:T(8,128)(2,1)}, u32[]{:S(2)}) copy-start(bf16[768,768]{1,0:T(8,128)(2,1)} %param.32) | copy-start | bytes 3538948
  7.2 273.5 %all-reduce.6.cloned.1.call-start = ((), (), s32[]{:S(2)}) async-start(), calls=%async_computation | async-start | bytes 393216
  68.1 39.6 %slice-start.3 = ((s8[4718592]{0:T(1024)(128)(4,1)}), s8[4194304]{0:T(1024)(128)(4,1)S(1)}, s32[]{:S(2)}) async-start(s8[4718592]{0:T(1024)(128)(4,1)} %bitcast.214), calls=%async_computation.5 | async-start | bytes 8388608
  69.8 37.9 %copy-start.7 = (f32[1024,768]{1,0:T(8,128)}, f32[1024,768]{1,0:T(8,128)S(1)}, u32[]{:S(2)}) copy-start(f32[1024,768]{1,0:T(8,128)S(1)} %get-tuple-element.299) | copy-start | bytes 9437188
  72.5 35.2 %slice-start.4 = ((s8[4718592]{0:T(1024)(128)(4,1)}), s8[524288]{0:T(1024)(128)(4,1)S(1)}, s32[]{:S(2)}) async-start(s8[4718592]{0:T(1024)(128)(4,1)} %bitcast.214), calls=%async_computation.6 | async-start | bytes 1048576
  72.5 35.3 %copy-start.63 = (f32[768]{0:T(1024)S(1)}, f32[768]{0:T(1024)}, u32[]{:S(2)}) copy-start(f32[768]{0:T(1024)} %param.39) | copy-start | bytes 9220
  107.7 5.5 copy-start.64
  113.3 45.6 %copy-start.52 = (s32[64]{0:T(128)S(1)}, s32[64]{0:T(128)}, u32[]{:S(2)}) copy-start(s32[64]{0:T(128)} %param.25) | copy-start | bytes 772
  113.3 46.5 %copy-start.50 = (s32[2]{0:T(128)S(1)}, s32[2]{0:T(128)}, u32[]{:S(2)}) copy-start(s32[2]{0:T(128)} %param.24) | copy-start | bytes 28
  113.3 46.5 %copy-start.51 = (f32[2]{0:T(128)S(1)}, f32[2]{0:T(128)}, u32[]{:S(2)}) copy-start(f32[2]{0:T(128)} %param.26) | copy-start | bytes 28
  114.1 171.4 %copy-start.43 = (f32[2,512]{1,0:T(2,128)S(1)}, f32[2,512]{1,0:T(2,128)}, u32[]{:S(2)}) copy-start(f32[2,512]{1,0:T(2,128)} %get-tuple-element.294) | copy-start | bytes 12292
  161.4 698.3 %all-reduce.8.cloned.1.call-start = ((), (), s32[]{:S(2)}) async-start(), calls=%async_computation.1 | async-start | bytes 56623104 | tf_op jit(solution)/shard_map/psum | solution.py:208
  280.7 5.9 copy-start.6
  299.8 17.5 %copy-start.8 = (f32[1024,768]{1,0:T(8,128)S(1)}, f32[1024,768]{1,0:T(8,128)}, u32[]{:S(2)}) copy-start(f32[1024,768]{1,0:T(8,128)} %copy-done.7) | copy-start | bytes 9437188
  317.3 11.0 %copy-start.14 = (bf16[1024,3072]{1,0:T(8,128)(2,1)S(1)}, bf16[1024,3072]{1,0:T(8,128)(2,1)}, u32[]{:S(2)}) copy-start(bf16[1024,3072]{1,0:T(8,128)(2,1)} %get-tuple-element.305) | copy-start | bytes 18874372
  317.3 11.0 %copy-start.20 = (f32[1024,768]{1,0:T(8,128)S(1)}, f32[1024,768]{1,0:T(8,128)}, u32[]{:S(2)}) copy-start(f32[1024,768]{1,0:T(8,128)} %get-tuple-element.292) | copy-start | bytes 9437188
  346.1 6.9 copy-start.3
  346.1 6.9 copy-start.33
  346.1 6.9 copy-start.35
  363.7 7.2 copy-start.25
  389.6 7.2 copy-start.25
  868.1 10.7 %slice-start = ((s8[9437184]{0:T(1024)(128)(4,1)}), s8[4194304]{0:T(1024)(128)(4,1)S(1)}, s32[]{:S(2)}) async-start(s8[9437184]{0:T(1024)(128)(4,1)} %bitcast.196), calls=%async_computation.2 | async-start | bytes 8388608
  869.5 9.3 %slice-start.1 = ((s8[9437184]{0:T(1024)(128)(4,1)}), s8[4194304]{0:T(1024)(128)(4,1)S(1)}, s32[]{:S(2)}) async-start(s8[9437184]{0:T(1024)(128)(4,1)} %bitcast.196), calls=%async_computation.3 | async-start | bytes 8388608
  869.5 9.3 %slice-start.2 = ((s8[9437184]{0:T(1024)(128)(4,1)}), s8[1048576]{0:T(1024)(128)(4,1)S(1)}, s32[]{:S(2)}) async-start(s8[9437184]{0:T(1024)(128)(4,1)} %bitcast.196), calls=%async_computation.4 | async-start | bytes 2097152
  (58 other events, 149.3 us)
Sparse Core Ops, SparseCore 0:
  161.5 119.0 all-reduce.5
  422.6 437.0 all-reduce.7
where the time goes:
time: 896 us; the launch traced here: 890 us
  waiting for transfers between devices  499 us (56%)
  matrix products  172 us (19%)
  blocking collectives  88.6 us (10%)
  local copies, waits for them, and re-layouts  75.6 us (8%)
  other arithmetic  37.8 us (4%)
  between operations  15.4 us (2%)
    psum x1, waiting for transfers between devices, per_device(): lax.psum((query_proj_grad, query_bias_grad, key_proj_grad, value_proj_gra...  380 us
    unnamed x3, waiting for transfers between devices  119 us
    psum x1, blocking collectives, per_device(): lax.psum((query_proj_grad, query_bias_grad, key_proj_grad, value_proj_gra...  44.9 us
    all_gather x1, blocking collectives, per_device(): every = lax.all_gather(pooled, 'dp', axis=0, tiled=True)  43.7 us
    dot_general x6, matrix products, ndot(): lax.dot_general(left, right, (((1,), (1,)), ((), ())), preferred_element_...  36 us
    dot_general x1, matrix products, per_device(): jnp.dot(first_low, expand_proj, preferred_element_type=jnp.float32)  35.2 us
    dot_general x6, matrix products, tdot(): lax.dot_general(left, right, (((0,), (0,)), ((), ())), preferred_element_...  32.3 us
    unnamed x141, local copies, waits for them, and re-layouts  31.5 us
  transfers between devices with their start and end apart: 2, of which 2 were waited for; matrix products, arithmetic and copies ran while one was open for 1% of the time, Pallas kernels for 0%

commit v1 on v0

--- a/solution.py
+++ b/solution.py
@@ -6,7 +6,413 @@
 from jax import lax
 from jax.sharding import PartitionSpec as P
 
+from jax.experimental import pallas as pl
+from jax.experimental.pallas import tpu as pltpu
+
 H = 12
+
+MESH = pl.DeviceIdType.MESH
+F32 = jnp.float32
+BF = jnp.bfloat16
+
+
+def rows16(index):
+    return pl.ds(pl.multiple_of(index * 16, 16), 16)
+
+
+def rows_at(start, size):
+    return pl.ds(pl.multiple_of(start, 8), size)
+
+
+def lanes_at(start, size):
+    return pl.ds(pl.multiple_of(start, 128), size)
+
+
+class Place:
+    def __init__(self):
+        me = lax.axis_index("dp")
+        self.me = me
+        self.c = me % 2
+        self.x = (me // 2) % 2
+        self.y = (me // 4) % 2
+        self.z = me // 8
+        self.sibling = me + 1 - 2 * self.c
+        self.to_x = me + 2 - 4 * self.x
+        self.to_y = me + 4 - 8 * self.y
+        self.up = me + 8
+        self.down = me - 8
+
+
+def stream_scratch():
+    return [
+        pltpu.VMEM((2, 64, 768), F32),
+        pltpu.VMEM((144, 128), F32),
+        pltpu.VMEM((2, 144, 128), F32),
+        pltpu.VMEM((144, 128), F32),
+        pltpu.VMEM((2, 144, 128), F32),
+        pltpu.VMEM((72, 128), F32),
+        pltpu.VMEM((2, 72, 128), F32),
+        pltpu.VMEM((72, 128), F32),
+        pltpu.VMEM((2, 72, 128), F32),
+        pltpu.VMEM((2, 192, 128), F32),
+        pltpu.VMEM((2, 2, 192, 128), F32),
+        pltpu.VMEM((128, 128), F32),
+        pltpu.VMEM((64, 128), F32),
+        pltpu.VMEM((4, 64, 128), F32),
+        pltpu.VMEM((4, 128, 128), F32),
+        pltpu.VMEM((16, 128), F32),
+        pltpu.VMEM((8, 128), F32),
+        pltpu.VMEM((8, 64, 768), F32),
+        pltpu.SemaphoreType.DMA((10, 2)),
+        pltpu.SemaphoreType.DMA((10, 2)),
+        pltpu.SemaphoreType.DMA((2,)),
+    ]
+
+
+N_STREAM_SCRATCH = 21
+
+
+class Stream:
+    def __init__(self, place, which, count, refs, grad_ref, grad_rows, out_ref, out_rows):
+        (self.sib_in, self.a_rs_out, self.a_rs_in, self.a_ag_out, self.a_ag_in, self.b_rs_out, self.b_rs_in,
+         self.b_ag_out, self.b_ag_in, self.z_out, self.z_in, self.p1, self.p2, self.p3, self.q1, self.q2, self.q3,
+         self.full, self.sent, self.came, self.kept) = refs
+        self.place = place
+        self.count = count
+        self.grad_ref = grad_ref
+        self.grad_rows = grad_rows
+        self.out_ref = out_ref
+        self.out_rows = out_rows
+        if which == 0:
+            self.d1, self.d2, self.to_a, self.to_b = place.x, place.y, place.to_x, place.to_y
+        else:
+            self.d1, self.d2, self.to_a, self.to_b = place.y, place.x, place.to_y, place.to_x
+
+    def prepare(self):
+        zero = jnp.zeros((192, 128), F32)
+        for side in range(2):
+            for parity in range(2):
+                self.z_in[side, parity] = zero
+
+    def copies(self, t):
+        place, n = self.place, self.count
+        par = t % 2
+        never = t < 0
+
+        def remote(i, src, dst, target):
+            return pltpu.make_async_remote_copy(
+                src_ref=src, dst_ref=dst, send_sem=self.sent.at[i, par], recv_sem=self.came.at[i, par],
+                device_id=(target,), device_id_type=MESH)
+
+        slot, row = self.grad_rows(t)
+        other = rows_at(row + 64 * (1 - place.c), 64)
+        m = t - 11
+        ring = lax.rem(t + 5, 8)
+        out_row = self.out_rows(m)
+        mine = rows_at(out_row + 64 * place.c, 64)
+        lead = (place.z, 3 - place.z)
+        zs = []
+        for side, device in ((0, place.up), (1, place.down)):
+            for half, when in ((0, (t >= 1) & (t < n + 5)), (1, (t >= 6) & (t < n + 10))):
+                for k in range(3):
+                    at, size = (0, 144 - 48 * k) if half == 0 else (144 - 48 * k, 48 + 48 * k)
+                    spot = pl.ds(at, size)
+                    copy = remote(5 + 2 * side + half, self.z_out.at[side, spot], self.z_in.at[side, par, spot], device)
+                    zs.append((copy, when, lead[side] == k, lead[side] == k + 1))
+        return [
+            (remote(0, self.grad_ref.at[slot, other], self.sib_in.at[par], place.sibling), (t >= 0) & (t < n), True, True),
+            (remote(1, self.a_rs_out, self.a_rs_in.at[par], self.to_a), (t >= 1) & (t < n + 4), True, True),
+            (remote(2, self.a_ag_out, self.a_ag_in.at[par], self.to_a), (t >= 7) & (t < n + 10), True, True),
+            (remote(3, self.b_rs_out, self.b_rs_in.at[par], self.to_b), (t >= 2) & (t < n + 5), True, True),
+            (remote(4, self.b_ag_out, self.b_ag_in.at[par], self.to_b), (t >= 6) & (t < n + 9), True, True),
+            (remote(9, self.full.at[ring], self.out_ref.at[mine], place.sibling), (t >= 11) & (t < n + 11), True, True),
+        ] + zs, (pltpu.make_async_copy(self.full.at[ring], self.out_ref.at[mine], self.kept.at[par]), (t >= 11) & (t < n + 11))
+
+    def start(self, t):
+        remote, (local, live) = self.copies(t)
+        for copy, when, sends, _ in remote:
+            pl.when(when if sends is True else when & sends)(copy.start)
+        pl.when(live)(local.start)
+
+    def wait(self, t):
+        remote, (local, live) = self.copies(t)
+        for copy, when, sends, takes in remote:
+            if sends is True:
+                @pl.when(when)
+                def _(copy=copy):
+                    copy.wait_send()
+                    copy.wait_recv()
+            else:
+                pl.when(when & sends)(copy.wait_send)
+                pl.when(when & takes)(copy.wait_recv)
+        pl.when(live)(local.wait)
+
+    def work(self, t):
+        place = self.place
+        z, d1, d2 = place.z, self.d1, self.d2
+        par = (t + 1) % 2
+        z_in, z_out = self.z_in, self.z_out
+        lead = (z, 3 - z)
+
+        def far(side, k):
+            return z - k if side == 0 else z + k
+
+        def target(side, step):
+            return z + 4 - step if side == 0 else z - 4 + step
+
+        def ring4(stage):
+            return lax.rem(t + 16 - stage, 4)
+
+        def ring8(stage):
+            return lax.rem(t + 16 - stage, 8)
+
+        def got_p(side, pos):
+            return z_in[side, par, 48 * pos:48 * pos + 16, :]
+
+        def got_q(side, pos, panel):
+            at = 48 * pos + 16 + 16 * panel
+            return z_in[side, par, at:at + 16, :]
+
+        def put_p(side, pos, value):
+            z_out[side, 48 * pos:48 * pos + 16, :] = value
+
+        def put_q(side, pos, panel, value):
+            at = 48 * pos + 16 + 16 * panel
+            z_out[side, at:at + 16, :] = value
+
+        def full_p(ring, block, value):
+            self.full[ring, rows16(block), lanes_at((2 * d1 + d2) * 128, 128)] = value
+
+        def full_q(ring, block, panel, value):
+            self.full[ring, rows16(block), 512 + 128 * panel:640 + 128 * panel] = value
+
+        @pl.when((t >= 11) & (t < self.count + 11))
+        def _stage11():
+            ring = ring8(11)
+            self.full[ring, :, lanes_at((1 - d1) * 256, 128)] = self.a_ag_in[par, 0:64, :]
+            self.full[ring, :, lanes_at((1 - d1) * 256 + 128, 128)] = self.a_ag_in[par, 64:128, :]
+            for side in range(2):
+                @pl.when(lead[side] == 3)
+                def _(side=side, ring=ring):
+                    for panel in range(2):
+                        full_q(ring, far(side, 3), panel, got_q(side, 1, panel))
+
+        @pl.when((t >= 10) & (t < self.count + 10))
+        def _stage10():
+            ring = ring8(10)
+            other = self.b_ag_in[par, 0:64, :]
+            self.full[ring, :, lanes_at((2 * d1 + 1 - d2) * 128, 128)] = other
+            self.a_ag_out[rows_at(64 * (1 - d2), 64), :] = other
+            self.a_ag_out[rows_at(64 * d2, 64), :] = self.full[ring, :, lanes_at((2 * d1 + d2) * 128, 128)]
+            for side in range(2):
+                @pl.when(lead[side] >= 2)
+                def _(side=side, ring=ring):
+                    for panel in range(2):
+                        value = got_q(side, 2, panel)
+                        full_q(ring, far(side, 2), panel, value)
+                        put_q(side, 1, panel, value)
+
+        @pl.when((t >= 9) & (t < self.count + 9))
+        def _stage9():
+            ring = ring8(9)
+            for side in range(2):
+                @pl.when(lead[side] == 3)
+                def _(side=side, ring=ring):
+                    full_p(ring, far(side, 3), got_p(side, 1))
+
+                @pl.when(lead[side] >= 1)
+                def _(side=side, ring=ring):
+                    for panel in range(2):
+                        value = got_q(side, 3, panel)
+                        full_q(ring, far(side, 1), panel, value)
+                        put_q(side, 2, panel, value)
+            self.b_ag_out[0:64, :] = self.full[ring, :, lanes_at((2 * d1 + d2) * 128, 128)]
+
+        @pl.when((t >= 8) & (t < self.count + 8))
+        def _stage8():
+            ring = ring8(8)
+            for side in range(2):
+                @pl.when(lead[side] >= 2)
+                def _(side=side, ring=ring):
+                    value = got_p(side, 2)
+                    full_p(ring, far(side, 2), value)
+                    put_p(side, 1, value)
+            self.full[ring, rows16(z), lanes_at(512 + 128 * (1 - d1), 128)] = self.a_ag_in[par, 128:144, :]
+            for panel in range(2):
+                value = self.full[ring, rows16(z), 512 + 128 * panel:640 + 128 * panel]
+                for side in range(2):
+                    put_q(side, 3, panel, value)
+
+        @pl.when((t >= 7) & (t < self.count + 7))
+        def _stage7():
+            ring = ring8(7)
+            for side in range(2):
+                @pl.when(lead[side] >= 1)
+                def _(side=side, ring=ring):
+                    value = got_p(side, 3)
+                    full_p(ring, far(side, 1), value)
+                    put_p(side, 2, value)
+            self.full[ring, rows_at(16 * z + 8 * (1 - d2), 8), lanes_at(512 + 128 * d1, 128)] = self.b_ag_in[par, 64:72, :]
+            self.a_ag_out[128:144, :] = self.full[ring, rows16(z), lanes_at(512 + 128 * d1, 128)]
+
+        @pl.when((t >= 6) & (t < self.count + 6))
+        def _stage6():
+            ring = ring8(6)
+            value = self.p3[ring4(6), rows16(z), :] + got_p(0, 0) + got_p(1, 0)
+            full_p(ring, z, value)
+            put_p(0, 3, value)
+            put_p(1, 3, value)
+            value = self.q3[...] + self.b_rs_in[par, 64:72, :]
+            self.full[ring, rows_at(16 * z + 8 * d2, 8), lanes_at(512 + 128 * d1, 128)] = value
+            self.b_ag_out[64:72, :] = value
+
+        @pl.when((t >= 5) & (t < self.count + 5))
+        def _stage5():
+            for side in range(2):
+                @pl.when(lead[side] <= 2)
+                def _(side=side):
+                    put_p(side, 0, self.p3[ring4(5), rows16(target(side, 3)), :] + got_p(side, 1))
+            self.q3[...] = self.q2[rows_at(8 * d2, 8), :] + self.a_rs_in[par, rows_at(128 + 8 * d2, 8), :]
+            self.b_rs_out[64:72, :] = self.q2[rows_at(8 * (1 - d2), 8), :] + self.a_rs_in[par, rows_at(128 + 8 * (1 - d2), 8), :]
+
+        @pl.when((t >= 4) & (t < self.count + 4))
+        def _stage4():
+            for side in range(2):
+                @pl.when(lead[side] <= 1)
+                def _(side=side):
+                    put_p(side, 1, self.p3[ring4(4), rows16(target(side, 2)), :] + got_p(side, 2))
+            ring = ring4(4)
+
+            def own_q(panel):
+                first = self.q1[ring, rows_at(64 * panel + 16 * z, 16), :]
+                spot = rows_at(16 + 16 * panel, 16)
+                return first + z_in[0, par, spot, :] + z_in[1, par, spot, :]
+
+            self.q2[...] = own_q(d1)
+            self.a_rs_out[128:144, :] = own_q(1 - d1)
+
+        @pl.when((t >= 3) & (t < self.count + 3))
+        def _stage3():
+            for side in range(2):
+                @pl.when(lead[side] <= 2)
+                def _(side=side):
+                    for panel in range(2):
+                        own = self.q1[ring4(3), rows_at(64 * panel + 16 * target(side, 3), 16), :]
+                        put_q(side, 0, panel, own + got_q(side, 1, panel))
+            ring = ring4(3)
+            self.p3[ring] = self.p2[...] + self.b_rs_in[par, 0:64, :]
+            for side in range(2):
+                @pl.when(lead[side] == 0)
+                def _(side=side, ring=ring):
+                    put_p(side, 2, self.p3[ring, rows16(target(side, 1)), :])
+
+        @pl.when((t >= 2) & (t < self.count + 2))
+        def _stage2():
+            for side in range(2):
+                @pl.when(lead[side] <= 1)
+                def _(side=side):
+                    for panel in range(2):
+                        own = self.q1[ring4(2), rows_at(64 * panel + 16 * target(side, 2), 16), :]
+                        put_q(side, 1, panel, own + got_q(side, 2, panel))
+            self.p2[...] = self.p1[rows_at(64 * d2, 64), :] + self.a_rs_in[par, rows_at(64 * d2, 64), :]
+            self.b_rs_out[0:64, :] = self.p1[rows_at(64 * (1 - d2), 64), :] + self.a_rs_in[par, rows_at(64 * (1 - d2), 64), :]
+
+        @pl.when((t >= 1) & (t < self.count + 1))
+        def _stage1():
+            slot, row = self.grad_rows(t - 1)
+            mine = rows_at(row + 64 * place.c, 64)
+
+            def summed(lane):
+                spot = lanes_at(lane, 128)
+                return self.grad_ref[slot, mine, spot] + self.sib_in[par, :, spot]
+
+            for half in range(2):
+                self.p1[64 * half:64 * half + 64, :] = summed(256 * d1 + 128 * half)
+                self.a_rs_out[64 * half:64 * half + 64, :] = summed(256 * (1 - d1) + 128 * half)
+            ring = ring4(1)
+            for panel in range(2):
+                self.q1[ring, 64 * panel:64 * panel + 64, :] = summed(512 + 128 * panel)
+            for side in range(2):
+                @pl.when(lead[side] == 0)
+                def _(side=side, ring=ring):
+                    for panel in range(2):
+                        put_q(side, 2, panel, self.q1[ring, rows_at(64 * panel + 16 * target(side, 1), 16), :])
+
+
+def greet_neighbours(place):
+    bar = pltpu.get_barrier_semaphore()
+
+    def hail(device):
+        pl.semaphore_signal(bar, 1, device_id=(device,), device_id_type=MESH)
+
+    hail(place.sibling)
+    hail(place.to_x)
+    hail(place.to_y)
+    pl.when(place.z < 3)(lambda: hail(place.up))
+    pl.when(place.z > 0)(lambda: hail(place.down))
+    ends = jnp.where(place.z == 0, 1, 0) + jnp.where(place.z == 3, 1, 0)
+    pl.semaphore_wait(bar, 5 - ends)
+
+
+def sum_kernel(g_ref, s_ref, o_ref, ring, loaded, *rest):
+    place = Place()
+    first, second = rest[:N_STREAM_SCRATCH], rest[N_STREAM_SCRATCH:]
+
+    def load(b):
+        slot = lax.rem(b, 2)
+        return pltpu.make_async_copy(g_ref.at[b], ring.at[slot], loaded.at[slot])
+
+    def chunk_rows(t, shift):
+        t = jnp.clip(t, 0, 36)
+        return lax.rem(t // 3, 2), lax.rem(t, 3) * 256 + shift
+
+    def out_rows(t, shift):
+        return jnp.clip(t, 0, 36) * 256 + shift
+
+    one = Stream(place, 0, 37, first, ring, lambda t: chunk_rows(t, 0), o_ref, lambda t: out_rows(t, 0))
+    two = Stream(place, 1, 36, second, ring, lambda t: chunk_rows(t, 128), o_ref, lambda t: out_rows(t, 128))
+    one.prepare()
+    two.prepare()
+    greet_neighbours(place)
+    load(jnp.int32(0)).start()
+
+    def step(t, carry):
+        b = t // 3
+
+        @pl.when((lax.rem(t, 3) == 0) & (b < 12))
+        def _():
+            load(b).wait()
+
+        @pl.when(t == 36)
+        def _():
+            ring[0, 0:128, :] = s_ref[...]
+
+        for stream in (one, two):
+            stream.wait(t - 1)
+            stream.work(t)
+            stream.start(t)
+
+        @pl.when((lax.rem(t, 3) == 1) & (b + 1 < 12))
+        def _():
+            load(b + 1).start()
+
+        return carry
+
+    lax.fori_loop(0, 49, step, 0)
+
+
+def sum_over_all(matrices, vectors):
+    small = jnp.pad(vectors, ((0, 116), (0, 0)))
+    return pl.pallas_call(
+        sum_kernel,
+        out_shape=jax.ShapeDtypeStruct((37 * 256 - 128, 768), F32),
+        in_specs=[pl.BlockSpec(memory_space=pl.ANY), pl.BlockSpec(memory_space=pltpu.VMEM)],
+        out_specs=pl.BlockSpec(memory_space=pl.ANY),
+        scratch_shapes=[pltpu.VMEM((2, 768, 768), F32), pltpu.SemaphoreType.DMA((2,))]
+        + stream_scratch() + stream_scratch(),
+        compiler_params=pltpu.CompilerParams(
+            collective_id=0, has_side_effects=True, vmem_limit_bytes=48 << 20),
+    )(matrices, small)
 
 
 def to_low(value):
@@ -63,6 +469,7 @@
     shrink_bias,
     second_gain,
     second_shift,
+    devices,
 ):
     sents = lengths.shape[0]
     rows_all = tokens.shape[0]
@@ -189,23 +596,24 @@
     tokens_grad = (
         ndot(dquery, query_proj) + ndot(dkey, key_proj) + ndot(dvalue, value_proj) + dfirst
     )
-    (
-        query_proj_grad,
-        query_bias_grad,
-        key_proj_grad,
-        value_proj_grad,
-        value_bias_grad,
-        mixer_proj_grad,
-        mixer_bias_grad,
-        first_gain_grad,
-        first_shift_grad,
-        expand_proj_grad,
-        expand_bias_grad,
-        shrink_proj_grad,
-        shrink_bias_grad,
-        second_gain_grad,
-        second_shift_grad,
-    ) = lax.psum(
+    if devices == 32 and width == 768 and expand_proj.shape[1] == 4 * width:
+        matrices = jnp.concatenate([
+            shrink_proj_grad.reshape(4, width, width),
+            expand_proj_grad.reshape(width, 4, width).transpose(1, 0, 2),
+            mixer_proj_grad[None], query_proj_grad[None], key_proj_grad[None], value_proj_grad[None]])
+        vectors = jnp.concatenate([
+            query_bias_grad, value_bias_grad, mixer_bias_grad, first_gain_grad, first_shift_grad,
+            shrink_bias_grad, second_gain_grad, second_shift_grad, expand_bias_grad]).reshape(12, width)
+        summed = sum_over_all(matrices, vectors)
+        blocks = summed[:12 * width].reshape(12, width, width)
+        small = summed[12 * width:12 * width + 12]
+        shrink_proj_grad = summed[:4 * width]
+        expand_proj_grad = blocks[4:8].transpose(1, 0, 2).reshape(width, 4 * width)
+        mixer_proj_grad, query_proj_grad, key_proj_grad, value_proj_grad = blocks[8], blocks[9], blocks[10], blocks[11]
+        (query_bias_grad, value_bias_grad, mixer_bias_grad, first_gain_grad, first_shift_grad,
+         shrink_bias_grad, second_gain_grad, second_shift_grad) = [small[i] for i in range(8)]
+        expand_bias_grad = small[8:].reshape(4 * width)
+    else:
         (
             query_proj_grad,
             query_bias_grad,
@@ -222,9 +630,26 @@
             shrink_bias_grad,
             second_gain_grad,
             second_shift_grad,
-        ),
-        "dp",
-    )
+        ) = lax.psum(
+            (
+                query_proj_grad,
+                query_bias_grad,
+                key_proj_grad,
+                value_proj_grad,
+                value_bias_grad,
+                mixer_proj_grad,
+                mixer_bias_grad,
+                first_gain_grad,
+                first_shift_grad,
+                expand_proj_grad,
+                expand_bias_grad,
+                shrink_proj_grad,
+                shrink_bias_grad,
+                second_gain_grad,
+                second_shift_grad,
+            ),
+            "dp",
+        )
     return (
         pair_scores,
         tokens_grad,
@@ -288,5 +713,5 @@
         P(),
     )
     return jax.shard_map(
-        per_device, mesh=mesh, in_specs=in_specs, out_specs=out_specs, check_vma=False
-    )
+        partial(per_device, devices=mesh.shape["dp"]), mesh=mesh, in_specs=in_specs, out_specs=out_specs, check_vma=False
+    )

time: 896 us -> 720 us (0.80)
  waiting for transfers between devices: 499 us -> 119 us
  Pallas kernels: 0 us -> 214 us
  blocking collectives: 88.6 us -> 43.7 us
  local copies, waits for them, and re-layouts: 75.6 us -> 102 us
  matrix products: 172 us -> 181 us
    psum x1 -> x0, waiting for transfers between devices: 380 us -> none  [per_device(): lax.psum((query_proj_grad, query_bias_grad, key_proj_grad, value_proj_gra...]
    pallas_call x0 -> x1, Pallas kernels: none -> 214 us  [sum_over_all(): pl.pallas_call(sum_kernel, out_shape=jax.ShapeDtypeStruct((37 * 256 - 128...]
    psum x1 -> x0, blocking collectives: 44.9 us -> none  [per_device(): lax.psum((query_proj_grad, query_bias_grad, key_proj_grad, value_proj_gra...]
    slice x0 -> x5, local copies, waits for them, and re-layouts: none -> 20.4 us  [the longest x1 11 us: per_device(): shrink_proj_grad = summed[:4 * width]]
    reshape x0 -> x4, local copies, waits for them, and re-layouts: none -> 15.6 us  [the longest x1 9.82 us: per_device(): expand_proj_grad.reshape(width, 4, width).transpose(1, 0, 2)]
    unnamed x141 -> x135, local copies, waits for them, and re-layouts: 31.5 us -> 21.2 us
    unnamed x3 -> x2, waiting for transfers between devices: 119 us -> 119 us
  transfers between devices with their start and end apart: 2 -> 1, of which waited for: 2 -> 1; matrix products, arithmetic and copies ran while one was open for 1% -> 0% of each run, Pallas kernels for 0% -> 0%
where the time goes in v1:
time: 720 us; the launch traced here: 714 us
  Pallas kernels  214 us (30%)
  matrix products  181 us (25%)
  waiting for transfers between devices  119 us (17%)
  local copies, waits for them, and re-layouts  102 us (14%)
  blocking collectives  43.7 us (6%)
  other arithmetic  37.8 us (5%)
  between operations  15.1 us (2%)
    pallas_call x1, Pallas kernels, sum_over_all(): pl.pallas_call(sum_kernel, out_shape=jax.ShapeDtypeStruct((37 * 256 - 128...  214 us
    unnamed x2, waiting for transfers between devices  119 us
    all_gather x1, blocking collectives, per_device(): every = lax.all_gather(pooled, 'dp', axis=0, tiled=True)  43.7 us
    dot_general x6, matrix products, ndot(): lax.dot_general(left, right, (((1,), (1,)), ((), ())), preferred_element_...  41.7 us
    dot_general x1, matrix products, per_device(): jnp.dot(first_low, expand_proj, preferred_element_type=jnp.float32)  35.4 us
    dot_general x6, matrix products, tdot(): lax.dot_general(left, right, (((0,), (0,)), ((), ())), preferred_element_...  34.9 us
    unnamed x135, local copies, waits for them, and re-layouts  21.2 us
    dot_general x2, matrix products, attend_back(): jnp.einsum('qhd,khd->hqk', dmix, value_rows, preferred_element_type=jnp.f...  14.8 us
  transfers between devices with their start and end apart: 1, of which 1 were waited for; matrix products, arithmetic and copies ran while one was open for 0% of the time, Pallas kernels for 0%

profile of v1, /device:TPU:0, one launch (start us, length us, event | category | flops | bytes accessed | tf_op | source)
XLA Modules:
  0.0 714.3 jit_solution(12475406762181746712)
XLA Ops:
  9.8 4.3 add_convert_fusion.2
  42.0 22.0 %while.26 = (s32[]{:T(128)}, bf16[2,512,12,64]{1,3,2,0:T(8,128)(2,1)}, f32[2,12,512]{2,1,0:T(8,128)S(1)}, bf16[2,512,12,64]{1,3,2,0:T(8,128)(2,1)}, pred[2,512]{...) while((s32[]{:T(128)}, ...), condition=%wide.region_3.4_spmd, body=%wide.region_0.3_spmd.sunk | while | flops 843048960 | bytes 48214648 | solution.py:512
  72.5 35.4 %multiply_convert_fusion.3 = (bf16[1024,3072]{1,0:T(8,128)(2,1)S(1)}, f32[1024,3072]{1,0:T(8,128)}, f32[1024,3072]{1,0:T(8,128)}) fusion(f32[3072]{0:T(1024)S(1)} %copy-done.56, bf16[768,3072]{1,0:T(8,128)(2,1)S(1)} %bitcast.236, f32[1024,768]{1,0:T(8,128)S(1)} %get-tuple-element.247, f32[768]{0:T(1024)S(1)} %copy-done.60, f32[768]{0:T(1024)S(1)} %copy-done.42, ...), kind=kOutput, calls=%fused_computation.65 | convolution fusion | flops 5043388416 | bytes 39348224 | tf_op jit(solution)/shard_map/dot_general | solution.py:519
  108.0 5.5 fusion.95
  115.2 43.7 %all-gather = f32[32,2,768]{2,1,0:T(2,128)S(1)} all-gather(f32[1,2,768]{2,1,0:T(2,128)S(1)} %fusion.133), channel_id=1, replica_groups=mesh['dp'=32] {'dp'}, dimensions={0}, use_global_device_ids=true | all-gather | bytes 202752 | tf_op jit(solution)/shard_map/all_gather | solution.py:529
  161.7 119.2 %all-reduce.4.cloned.1.call-done = f32[64,768]{1,0:T(8,128)} async-done(((f32[64,768]{1,0:T(8,128)}), f32[64,768]{1,0:T(8,128)}) %all-reduce.4.cloned.1.call-update) | async-done | bytes 196624
  289.9 10.1 %fusion.98 = f32[3072,768]{1,0:T(8,128)} fusion(bf16[1024,3072]{1,0:T(8,128)(2,1)} %copy-done.61, bf16[1024,768]{1,0:T(8,128)(2,1)S(1)} %get-tuple-element.219), kind=kOutput, calls=%fused_computation.187 | convolution fusion | flops 4831838208 | bytes 17301504 | tf_op jit(solution)/shard_map/dot_general | solution.py:423
  300.0 17.5 %convert_reduce_fusion = (f32[3072]{0:T(1024)}, bf16[1024,3072]{1,0:T(8,128)(2,1)}) fusion(f32[1024,3072]{1,0:T(8,128)} %get-tuple-element.229, bf16[1024,768]{1,0:T(8,128)(2,1)S(1)} %get-tuple-element.219, bf16[3072,768]{1,0:T(8,128)(2,1)} %param.38, f32[1024,3072]{1,0:T(8,128)} %get-tuple-element.248, f32[3072]{0:T(1024)S(1)} %copy-done.56), kind=kOutput, calls=%fused_computation.63 | convolution fusion | flops 4885312512 | bytes 37773312 | tf_op jit(solution)/shard_map/dot_general | solution.py:429
  317.5 13.3 %fusion.84 = f32[768,3072]{0,1:T(8,128)} fusion(bf16[1024,3072]{1,0:T(8,128)(2,1)} %get-tuple-element.253, f32[1024,768]{1,0:T(8,128)S(1)} %copy-done.12, f32[768]{0:T(1024)S(1)} %copy-done.60, f32[768]{0:T(1024)S(1)} %copy-done.42, f32[1024]{0:T(1024)S(1)} %add_rsqrt_fusion.1, f32[1024]{0:T(1024)S(1)} %broadcast_multiply_fusion.4), kind=kOutput, calls=%fused_computation.178 | convolution fusion | flops 4835770368 | bytes 18888704 | tf_op jit(solution)/shard_map/dot_general | solution.py:423
  330.8 9.0 %multiply_reduce_fusion.2 = (f32[768]{0:T(1024)}, f32[1024]{0:T(1024)S(1)}, f32[1024]{0:T(1024)S(1)}, f32[768]{0:T(1024)}, f32[1024,768]{1,0:T(8,128)S(1)}) fusion(f32[1024,768]{1,0:T(8,128)S(1)} %copy-done.12, f32[1024]{0:T(1024)S(1)} %add_rsqrt_fusion.1, f32[1024]{0:T(1024)S(1)} %broadcast_multiply_fusion.4, f32[768]{0:T(1024)S(1)} %copy-done.42, ...), kind=kOutput, calls=%fused_computation.94 | convolution fusion | flops 4839698432 | bytes 20472832 | tf_op jit(solution)/shard_map/dot_general | solution.py:429
  353.2 52.4 %while.27 = (s32[]{:T(128)}, bf16[2,512,12,64]{1,3,2,0:T(8,128)(2,1)}, bf16[2,512,12,64]{1,3,2,0:T(8,128)(2,1)}, bf16[2,512,12,64]{1,3,2,0:T(8,128)(2,1)}, bf16[...) while((s32[]{:T(128)}, ...), condition=%wide.region_19.20_spmd, body=%wide.region_17.19_spmd.sunk | while | flops 2062411776 | bytes 146472784 | solution.py:587
  356.8 7.4 %multiply_reduce_fusion.11 = (f32[12,512]{1,0:T(8,128)S(1)}, f32[12,512,512]{1,2,0:T(8,128)}) fusion(f32[12,512,512]{1,2,0:T(8,128)S(1)} %fusion.160, f32[12,512]{1,0:T(8,128)S(1)} %dynamic-slice_bitcast_fusion.2, pred[512]{0:T(512)(128)(4,1)S(1)} %dynamic-slice_reduce_fusion.5, bf16[2,512,12,64]{1,3,2,0:T(8,128)(2,1)S(1)} %copy-done.9, ...), kind=kOutput, calls=%fused_computation.22.clone.1 | convolution fusion | flops 418375680 | bytes 26797568 | tf_op jit(solution)/shard_map/while/body/eval_jaxpr/qhd,khd->hqk/dot_general | solution.py:574
  364.2 7.2 %multiply_convert_fusion.5 = bf16[12,512,512]{1,2,0:T(8,128)(2,1)S(1)} fusion(f32[12,512,512]{1,2,0:T(8,128)} %get-tuple-element.366, f32[12,512,512]{1,2,0:T(8,128)S(1)} %fusion.160, f32[12,512]{1,0:T(8,128)S(1)} %get-tuple-element.367, f32[12,512]{1,0:T(8,128)S(1)} %dynamic-slice_bitcast_fusion.2, pred[512]{0:T(512)(128)(4,1)S(1)} %dynamic-slice_reduce_fusion.5), kind=kLoop, calls=%fused_computation.21.clone.1 | loop fusion | flops 18874368 | bytes 31506944 | tf_op jit(solution)/shard_map/while/body/eval_jaxpr/convert_element_type | solution.py:419
  382.8 7.4 %multiply_reduce_fusion.11 = (f32[12,512]{1,0:T(8,128)S(1)}, f32[12,512,512]{1,2,0:T(8,128)}) fusion(f32[12,512,512]{1,2,0:T(8,128)S(1)} %fusion.160, f32[12,512]{1,0:T(8,128)S(1)} %dynamic-slice_bitcast_fusion.2, pred[512]{0:T(512)(128)(4,1)S(1)} %dynamic-slice_reduce_fusion.5, bf16[2,512,12,64]{1,3,2,0:T(8,128)(2,1)S(1)} %copy-done.9, ...), kind=kOutput, calls=%fused_computation.22.clone.1 | convolution fusion | flops 418375680 | bytes 26797568 | tf_op jit(solution)/shard_map/while/body/eval_jaxpr/qhd,khd->hqk/dot_general | solution.py:574
  390.2 7.2 %multiply_convert_fusion.5 = bf16[12,512,512]{1,2,0:T(8,128)(2,1)S(1)} fusion(f32[12,512,512]{1,2,0:T(8,128)} %get-tuple-element.366, f32[12,512,512]{1,2,0:T(8,128)S(1)} %fusion.160, f32[12,512]{1,0:T(8,128)S(1)} %get-tuple-element.367, f32[12,512]{1,0:T(8,128)S(1)} %dynamic-slice_bitcast_fusion.2, pred[512]{0:T(512)(128)(4,1)S(1)} %dynamic-slice_reduce_fusion.5), kind=kLoop, calls=%fused_computation.21.clone.1 | loop fusion | flops 18874368 | bytes 31506944 | tf_op jit(solution)/shard_map/while/body/eval_jaxpr/convert_element_type | solution.py:419
  407.4 4.2 copy.92
  413.9 9.8 %copy.96 = f32[768,4,768]{2,0,1:T(8,128)} copy(f32[768,4,768]{0,2,1:T(8,128)} %bitcast.215) | data formatting | bytes 18874368 | tf_op jit(solution)/shard_map/reshape | solution.py:602
  423.8 8.7 %constant_dynamic-update-slice_fusion = f32[12,768,768]{2,1,0:T(8,128)} fusion(f32[4,768,768]{2,1,0:T(8,128)} %bitcast.214), kind=kLoop, calls=%fused_computation.121 | loop fusion | bytes 18874368
  432.4 4.7 bitcast_dynamic-update-slice_fusion.2
  453.1 214.2 %shard_map.314 = f32[9344,768]{1,0:T(8,128)} custom-call(f32[12,768,768]{2,1,0:T(8,128)} %bitcast_dynamic-update-slice_fusion.3.g_ref, f32[128,768]{1,0:T(8,128)S(1)} %pad.4.s_ref), custom_call_target="tpu_custom_call" | custom-call | tf_op jit(solution)/shard_map/pallas_call | solution.py:406
  667.3 11.0 %fusion.92 = (f32[3072,768]{1,0:T(8,128)}, f32[3072,768]{1,0:T(8,128)S(1)}) fusion(f32[9344,768]{1,0:T(8,128)} %shard_map.314), kind=kLoop, calls=%fused_computation.181 | loop fusion | bytes 37748736 | tf_op jit(solution)/shard_map/slice | solution.py:610
  678.3 7.7 %fusion.93 = (f32[768,768]{1,0:T(8,128)}, f32[768,768]{1,0:T(8,128)}, f32[768,768]{1,0:T(8,128)}, f32[768,768]{1,0:T(8,128)}) fusion(f32[9344,768]{1,0:T(8,128)} %shard_map.314), kind=kLoop, calls=%fused_computation.182 | loop fusion | bytes 18874368 | tf_op jit(solution)/shard_map/slice | solution.py:612
  694.0 5.2 copy.109
  699.8 7.4 %add_add_fusion = f32[1024,768]{1,0:T(8,128)} fusion(f32[1024,768]{1,0:T(8,128)} %copy-done.13, f32[1024,768]{1,0:T(8,128)} %fusion.96, f32[1024,768]{1,0:T(8,128)} %fusion.97, bf16[1024,768]{0,1:T(8,128)(2,1)S(1)} %bitcast.220, bf16[768,768]{1,0:T(8,128)(2,1)} %param.30), kind=kOutput, calls=%fused_computation.98 | convolution fusion | flops 1210318848 | bytes 15335424 | tf_op jit(solution)/shard_map/dot_general | solution.py:429
  (259 shorter events, 138.1 us)
Async XLA Ops:
  7.2 60.9 %copy-start = (bf16[768,768]{1,0:T(8,128)(2,1)S(1)}, bf16[768,768]{1,0:T(8,128)(2,1)}, u32[]{:S(2)}) copy-start(bf16[768,768]{1,0:T(8,128)(2,1)} %param.32) | copy-start | bytes 3538948
  7.2 273.7 %all-reduce.4.cloned.1.call-start = ((), (), s32[]{:S(2)}) async-start(), calls=%async_computation | async-start | bytes 393216
  68.1 39.8 %slice-start.1 = ((s8[4718592]{0:T(1024)(128)(4,1)}), s8[4194304]{0:T(1024)(128)(4,1)S(1)}, s32[]{:S(2)}) async-start(s8[4718592]{0:T(1024)(128)(4,1)} %bitcast.233), calls=%async_computation.2 | async-start | bytes 8388608
  69.8 38.1 %copy-start.11 = (f32[1024,768]{1,0:T(8,128)}, f32[1024,768]{1,0:T(8,128)S(1)}, u32[]{:S(2)}) copy-start(f32[1024,768]{1,0:T(8,128)S(1)} %get-tuple-element.247) | copy-start | bytes 9437188
  72.5 35.5 %slice-start.2 = ((s8[4718592]{0:T(1024)(128)(4,1)}), s8[524288]{0:T(1024)(128)(4,1)S(1)}, s32[]{:S(2)}) async-start(s8[4718592]{0:T(1024)(128)(4,1)} %bitcast.233), calls=%async_computation.3 | async-start | bytes 1048576
  72.5 35.5 %copy-start.59 = (f32[768]{0:T(1024)S(1)}, f32[768]{0:T(1024)}, u32[]{:S(2)}) copy-start(f32[768]{0:T(1024)} %param.39) | copy-start | bytes 9220
  113.5 45.6 %copy-start.47 = (s32[64]{0:T(128)S(1)}, s32[64]{0:T(128)}, u32[]{:S(2)}) copy-start(s32[64]{0:T(128)} %param.25) | copy-start | bytes 772
  113.5 46.5 %copy-start.45 = (s32[2]{0:T(128)S(1)}, s32[2]{0:T(128)}, u32[]{:S(2)}) copy-start(s32[2]{0:T(128)} %param.24) | copy-start | bytes 28
  113.5 46.5 %copy-start.46 = (f32[2]{0:T(128)S(1)}, f32[2]{0:T(128)}, u32[]{:S(2)}) copy-start(f32[2]{0:T(128)} %param.26) | copy-start | bytes 28
  114.3 171.3 %copy-start.37 = (f32[2,512]{1,0:T(2,128)S(1)}, f32[2,512]{1,0:T(2,128)}, u32[]{:S(2)}) copy-start(f32[2,512]{1,0:T(2,128)} %get-tuple-element.242) | copy-start | bytes 12292
  280.9 5.9 copy-start.6
  300.0 17.5 %copy-start.12 = (f32[1024,768]{1,0:T(8,128)S(1)}, f32[1024,768]{1,0:T(8,128)}, u32[]{:S(2)}) copy-start(f32[1024,768]{1,0:T(8,128)} %copy-done.11) | copy-start | bytes 9437188
  317.5 13.3 %copy-start.21 = (f32[1024,768]{1,0:T(8,128)S(1)}, f32[1024,768]{1,0:T(8,128)}, u32[]{:S(2)}) copy-start(f32[1024,768]{1,0:T(8,128)} %get-tuple-element.240) | copy-start | bytes 9437188
  317.5 13.3 %copy-start.62 = (bf16[1024,3072]{1,0:T(8,128)(2,1)S(1)}, bf16[1024,3072]{1,0:T(8,128)(2,1)}, u32[]{:S(2)}) copy-start(bf16[1024,3072]{1,0:T(8,128)(2,1)} %get-tuple-element.253) | copy-start | bytes 18874372
  346.3 6.9 copy-start.3
  346.3 6.9 copy-start.28
  346.3 6.9 copy-start.30
  364.2 7.2 %copy-start.24 = (bf16[2,512,12,64]{1,3,2,0:T(8,128)(2,1)S(1)}, bf16[2,512,12,64]{1,3,2,0:T(8,128)(2,1)}, u32[]{:S(2)}) copy-start(bf16[2,512,12,64]{1,3,2,0:T(8,128)(2,1)} %get-tuple-element.405) | copy-start | bytes 4718596 | tf_op jit(solution)/shard_map/while
  390.2 7.2 %copy-start.24 = (bf16[2,512,12,64]{1,3,2,0:T(8,128)(2,1)S(1)}, bf16[2,512,12,64]{1,3,2,0:T(8,128)(2,1)}, u32[]{:S(2)}) copy-start(bf16[2,512,12,64]{1,3,2,0:T(8,128)(2,1)} %get-tuple-element.405) | copy-start | bytes 4718596 | tf_op jit(solution)/shard_map/while
  405.6 6.0 copy-start.17
  423.8 8.7 %copy-start.7 = (f32[768,4,768]{2,0,1:T(8,128)S(1)}, f32[768,4,768]{2,0,1:T(8,128)}, u32[]{:S(2)}) copy-start(f32[768,4,768]{2,0,1:T(8,128)} %copy.96) | copy-start | bytes 28311556
  443.8 6.4 copy-start.19
  678.3 9.4 %copy-start.53 = (bf16[768,768]{1,0:T(8,128)(2,1)S(1)}, bf16[768,768]{1,0:T(8,128)(2,1)}, u32[]{:S(2)}) copy-start(bf16[768,768]{1,0:T(8,128)(2,1)} %param.27) | copy-start | bytes 3538948
  699.8 7.4 %copy-start.1 = (bf16[768,768]{1,0:T(8,128)(2,1)S(1)}, bf16[768,768]{1,0:T(8,128)(2,1)}, u32[]{:S(2)}) copy-start(bf16[768,768]{1,0:T(8,128)(2,1)} %param.32) | copy-start | bytes 3538948
  (53 other events, 142.3 us)
Sparse Core Ops, SparseCore 0:
  161.7 119.1 all-reduce.3

commit v2 on v1

--- a/solution.py
+++ b/solution.py
@@ -339,28 +339,335 @@
                         put_q(side, 2, panel, self.q1[ring, rows_at(64 * panel + 16 * target(side, 1), 16), :])
 
 
-def greet_neighbours(place):
-    bar = pltpu.get_barrier_semaphore()
-
-    def hail(device):
-        pl.semaphore_signal(bar, 1, device_id=(device,), device_id_type=MESH)
-
-    hail(place.sibling)
-    hail(place.to_x)
-    hail(place.to_y)
-    pl.when(place.z < 3)(lambda: hail(place.up))
-    pl.when(place.z > 0)(lambda: hail(place.down))
-    ends = jnp.where(place.z == 0, 1, 0) + jnp.where(place.z == 3, 1, 0)
-    pl.semaphore_wait(bar, 5 - ends)
-
-
-def sum_kernel(g_ref, s_ref, o_ref, ring, loaded, *rest):
+T0 = (((0,), (0,)), ((), ()))
+NT = (((1,), (1,)), ((), ()))
+
+
+def mm(left, right):
+    return jnp.dot(left, right, preferred_element_type=F32)
+
+
+def mm_nt(left, right):
+    return lax.dot_general(left, right, NT, preferred_element_type=F32)
+
+
+def mm_t(left, right):
+    return lax.dot_general(left, right, T0, preferred_element_type=F32)
+
+
+def row_of(ref):
+    return ref[...].reshape(1, -1)
+
+
+def normal_cdf(pre):
+    size = jnp.abs(pre)
+    down = 1.0 + (0.3275911 / 1.4142135623730951) * size
+    t = pl.reciprocal(down, approx=True)
+    t = t * (2.0 - down * t)
+    bell = jnp.exp(-0.5 * pre * pre)
+    poly = t * (0.5 * 0.254829592 + t * (0.5 * -0.284496736 + t * (0.5 * 1.421413741 + t * (
+        0.5 * -1.453152027 + t * (0.5 * 1.061405429)))))
+    tail = poly * bell
+    return jnp.where(pre >= 0, 1.0 - tail, tail), bell
+
+
+G0, D0 = 0, 4
+X, Q, K, V, O, Y1, DZ, DA, DO = 8, 9, 10, 11, 12, 13, 14, 15, 16
+N_ACTS = 17
+
+
+class Net:
+    def __init__(self, **refs):
+        self.__dict__.update(refs)
+
+    def project(self, i):
+        rows = pl.ds(pl.multiple_of(i * 256, 256), 256)
+        acts = self.acts
+        x = acts[X, rows, :]
+        acts[Q, rows, :] = (mm(x, self.w_q[...]) + row_of(self.query_bias)).astype(BF) * BF(0.125)
+        acts[K, rows, :] = mm(x, self.w_k[...]).astype(BF)
+        acts[V, rows, :] = (mm(x, self.w_v[...]) + row_of(self.value_bias)).astype(BF)
+
+    def masks(self):
+        place = lax.broadcasted_iota(jnp.int32, (8, 512), 1)
+        for s in range(2):
+            self.key_row[s] = jnp.where(place < self.lengths[s], 0.0, -1e9)
+
+    def attend(self, i):
+        s, pair = i // 6, lax.rem(i, 6)
+        rows = pl.ds(pl.multiple_of(s * 512, 512), 512)
+        lanes = lanes_at(pair * 128, 128)
+        acts = self.acts
+        k = acts[K, rows, lanes]
+        v = acts[V, rows, lanes]
+        lane = lax.broadcasted_iota(jnp.int32, (1, 128), 1)
+        v_ones = jnp.concatenate([v, jnp.ones((512, 128), BF)], axis=1)
+        step = 256
+        for part in range(512 // step):
+            some = pl.ds(pl.multiple_of(s * 512 + part * step, step), step)
+            q = acts[Q, some, lanes]
+            outs = []
+            tops = []
+            for head in range(2):
+                live = (lane >= 64) if head else (lane < 64)
+                score = mm_nt(jnp.where(live, q, BF(0)), k) + self.key_row[s, 0:1, :]
+                top = jnp.max(score, axis=1, keepdims=True)
+                e = jnp.exp(score - top).astype(BF)
+                both = mm(e, v_ones)
+                total = both[:, 128:]
+                outs.append(both[:, :128] / total)
+                tops.append(top + jnp.log(total))
+            acts[O, some, lanes] = jnp.where(lane < 64, outs[0], outs[1]).astype(BF)
+            spot = pl.ds(part * step, step)
+            old = self.logs[s, spot, :]
+            old = jnp.where(lane == 2 * pair, tops[0], old)
+            self.logs[s, spot, :] = jnp.where(lane == 2 * pair + 1, tops[1], old)
+
+    def normed(self, rows):
+        mean = jnp.sum(rows, axis=1, keepdims=True) * (1.0 / 768)
+        centred = rows - mean
+        spread = jnp.sum(centred * centred, axis=1, keepdims=True) * (1.0 / 768)
+        inverse = lax.rsqrt(spread + 1e-6)
+        return centred * inverse, inverse
+
+    def feed(self, i):
+        rows = pl.ds(pl.multiple_of(i * 256, 256), 256)
+        acts = self.acts
+        h1 = acts[X, rows, :].astype(F32) + mm(acts[O, rows, :], self.w_m[...]) + row_of(self.mixer_bias)
+        n1, r1 = self.normed(h1)
+        self.n1[rows, :] = n1.astype(self.n1.dtype)
+        self.r1[rows, :] = jnp.broadcast_to(r1, (256, 128))
+        y1 = n1 * row_of(self.first_gain) + row_of(self.first_shift)
+        self.z[...] = y1 + row_of(self.shrink_bias)
+        acts[Y1, rows, :] = y1.astype(BF)
+        for j in range(4):
+            self.feed_block(rows, j)
+        n2, r2 = self.normed(self.z[...])
+        self.n2[rows, :] = n2
+        self.r2[rows, :] = jnp.broadcast_to(r2, (256, 128))
+        s = i // 2
+        at = lax.broadcasted_iota(jnp.int32, (256, 1), 0) + lax.rem(i, 2) * 256
+        live = jnp.where(at < self.lengths[s], n2, 0.0)
+        part = jnp.sum(live, axis=0, keepdims=True)
+        first = lax.rem(i, 2) == 0
+        self.n2_sum[s, 0:1, :] = jnp.where(first, part, self.n2_sum[s, 0:1, :] + part)
+
+    def feed_block(self, rows, j):
+        acts = self.acts
+        cols = pl.ds(768 * j, 768)
+        pre = mm(acts[Y1, rows, :], self.w_e[:, cols]) + self.expand_bias[cols].reshape(1, 768)
+        cdf, bell = normal_cdf(pre)
+        low = (pre * cdf).astype(BF)
+        acts[G0 + j, rows, :] = low
+        acts[D0 + j, rows, :] = (cdf + pre * bell * 0.3989422804014327).astype(BF)
+        self.z[...] += mm(low, self.w_s[cols, :])
+
+    def pool(self, s):
+        count = self.lengths[s].astype(F32)
+        return self.n2_sum[s, 0:1, :] * row_of(self.second_gain) / count + row_of(self.second_shift)
+
+
+class Back(Net):
+    def turn_logs(self):
+        for s in range(2):
+            self.logs_t[s] = jnp.transpose(self.logs[s])[0:16, :]
+
+    def gather(self, place):
+        c, chip = place.c, place.me // 2
+        every = self.every
+        for s in range(2):
+            u = self.pool(s)
+            for j in range(6):
+                every[c, chip, 8 * s + j:8 * s + j + 1, :] = u[:, 128 * j:128 * j + 128]
+            every[c, chip, 8 * s + 6:8 * s + 8, :] = jnp.full((2, 128), self.targets[s], F32)
+
+        def copy(source, device):
+            return pltpu.make_async_remote_copy(
+                src_ref=every.at[c, source], dst_ref=every.at[c, source], send_sem=self.told.at[device // 2],
+                recv_sem=self.heard.at[source], device_id=(device,), device_id_type=MESH)
+
+        def out(k, carry):
+            copy(chip, lax.rem(chip + k, 16) * 2 + c).start()
+            return carry
+
+        def done(k, carry):
+            copy(chip, lax.rem(chip + k, 16) * 2 + c).wait_send()
+            copy(lax.rem(chip + 16 - k, 16), place.me).wait_recv()
+            return carry
+
+        lax.fori_loop(1, 16, out, 0)
+        lax.fori_loop(1, 16, done, 0)
+        share = pltpu.make_async_remote_copy(
+            src_ref=every.at[c], dst_ref=every.at[c], send_sem=self.told.at[chip],
+            recv_sem=self.heard.at[chip], device_id=(place.sibling,), device_id_type=MESH)
+        share.start()
+        share.wait_send()
+        share.wait_recv()
+
+    def pair(self, place, s):
+        here = place.me * 2 + s
+        wanted = jnp.full((8, 128), self.partners[here], jnp.int32)
+        mine = self.every[place.c, place.me // 2, 8 * s:8 * s + 8, :]
+
+        def pick(i, found):
+            far, near = found
+            device = i // 2
+            tile = self.every[lax.rem(device, 2), device // 2, rows_at(8 * lax.rem(i, 2), 8), :]
+            far += jnp.where(wanted == i, tile, 0.0)
+            near += jnp.where(jnp.full((8, 128), self.partners[i], jnp.int32) == here, tile, 0.0)
+            return far, near
+
+        nothing = jnp.zeros((8, 128), F32)
+        far, near = lax.fori_loop(0, 64, pick, (nothing, nothing))
+        live = lax.broadcasted_iota(jnp.int32, (8, 128), 0) < 6
+
+        def inner(left, right):
+            return jnp.sum(jnp.where(live, left * right, 0.0), axis=(0, 1), keepdims=True)
+
+        length = jnp.sqrt(inner(mine, mine) + 1e-6)
+        far_length = jnp.sqrt(inner(far, far) + 1e-6)
+        near_length = jnp.sqrt(inner(near, near) + 1e-6)
+        score = inner(mine, far) / (length * far_length)
+        near_score = inner(near, mine) / (near_length * length)
+        miss = score - mine[6:7, 0:1]
+        near_miss = near_score - near[6:7, 0:1]
+        own = mine / (length * length)
+        grad = miss * (far / (length * far_length) - score * own)
+        grad += near_miss * (near / (near_length * length) - near_score * own)
+        for j in range(6):
+            self.du[s, 0:1, 128 * j:128 * j + 128] = grad[j:j + 1, :]
+        self.scores[s] = jnp.sum(score)
+
+    def clear(self):
+        self.vec[...] = jnp.zeros_like(self.vec)
+
+    def add_vec(self, at, rows):
+        self.vec[at:at + 1, :] += jnp.sum(rows.astype(F32), axis=0, keepdims=True)
+
+    def second_vectors(self):
+        gain = jnp.zeros((1, 768), F32)
+        for s in range(2):
+            gain += self.du[s, 0:1, :] * self.n2_sum[s, 0:1, :] / self.lengths[s].astype(F32)
+        self.vec[6:7, :] = gain
+        self.vec[7:8, :] = self.du[0, 0:1, :] + self.du[1, 0:1, :]
+
+    def back_second(self, i):
+        rows = pl.ds(pl.multiple_of(i * 256, 256), 256)
+        s = i // 2
+        up = self.du[s, 0:1, :] * row_of(self.second_gain) / self.lengths[s].astype(F32)
+        mean = jnp.sum(up, axis=1, keepdims=True) * (1.0 / 768)
+        n2 = self.n2[rows, :]
+        along = jnp.sum(n2 * up, axis=1, keepdims=True) * (1.0 / 768)
+        at = lax.broadcasted_iota(jnp.int32, (256, 1), 0) + lax.rem(i, 2) * 256
+        dh2 = jnp.where(at < self.lengths[s], self.r2[rows, 0:1] * (up - mean - n2 * along), 0.0)
+        self.n2[rows, :] = dh2
+        dz = dh2.astype(BF)
+        self.acts[DZ, rows, :] = dz
+        self.add_vec(5, dz)
+
+    def back_hidden(self, i):
+        j, half = i // 2, lax.rem(i, 2)
+        rows = pl.ds(pl.multiple_of(half * 512, 512), 512)
+        units = pl.ds(pl.multiple_of(j * 768, 768), 768)
+        df = (mm_nt(self.acts[DZ, rows, :], self.w_s[units, :]) * self.acts[D0 + j, rows, :].astype(F32)).astype(BF)
+        self.acts[D0 + j, rows, :] = df
+        part = jnp.sum(df.astype(F32), axis=0, keepdims=True)
+        line = lax.broadcasted_iota(jnp.int32, (8, 768), 0) == j
+        self.vec[8:16, :] += jnp.where(line, part, 0.0)
+
+    def back_first(self, i):
+        rows = pl.ds(pl.multiple_of(i * 256, 256), 256)
+        acts = self.acts
+        up = self.n2[rows, :]
+        for j in range(4):
+            up += mm_nt(acts[D0 + j, rows, :], self.w_e[:, 768 * j:768 * j + 768])
+        n1 = self.n1[rows, :].astype(F32)
+        self.add_vec(3, up * n1)
+        self.add_vec(4, up)
+        dn = up * row_of(self.first_gain)
+        mean = jnp.sum(dn, axis=1, keepdims=True) * (1.0 / 768)
+        along = jnp.sum(dn * n1, axis=1, keepdims=True) * (1.0 / 768)
+        dh1 = self.r1[rows, 0:1] * (dn - mean - n1 * along)
+        self.n2[rows, :] = dh1
+        da = dh1.astype(BF)
+        acts[DA, rows, :] = da
+        self.add_vec(2, da)
+        acts[DO, rows, :] = mm_nt(da, self.w_m[...]).astype(BF)
+
+    def attend_back(self, i):
+        s, head = i // 12, lax.rem(i, 12)
+        rows = pl.ds(pl.multiple_of(s * 512, 512), 512)
+        lanes = lanes_at((head // 2) * 128, 128)
+        acts = self.acts
+        lane = lax.broadcasted_iota(jnp.int32, (1, 128), 1)
+        live = (lane // 64) == lax.rem(head, 2)
+        q_all, k, v = acts[Q, rows, lanes], acts[K, rows, lanes], acts[V, rows, lanes]
+        q = jnp.where(live, q_all, BF(0))
+        up = jnp.where(live, acts[DO, rows, lanes], BF(0))
+        place = lax.broadcasted_iota(jnp.int32, (512, 1), 0)
+        off = jnp.where(place < self.lengths[s], 0.0, -1e9)
+        probs = jnp.exp(mm_nt(k, q) + off - self.logs_t[s, pl.ds(head, 1), :])
+        weighed = probs * mm_nt(v, up)
+        delta = jnp.sum(weighed, axis=0, keepdims=True)
+        ds = (weighed - probs * delta).astype(BF)
+        dv = mm(probs.astype(BF), up)
+        dk = mm(ds, q)
+        dq = mm_t(ds, k) * 0.125
+        acts[Q, rows, lanes] = jnp.where(live, dq.astype(BF), q_all)
+        acts[K, rows, lanes] = jnp.where(live, dk.astype(BF), k)
+        acts[V, rows, lanes] = jnp.where(live, dv.astype(BF), v)
+
+    def token_copy(self, i):
+        rows = pl.ds(pl.multiple_of(i * 256, 256), 256)
+        return pltpu.make_async_copy(self.n2.at[rows], self.tokens_grad.at[rows], self.wrote.at[i])
+
+    def back_tokens(self, i):
+        rows = pl.ds(pl.multiple_of(i * 256, 256), 256)
+        dq, dk, dv = self.acts[Q, rows, :], self.acts[K, rows, :], self.acts[V, rows, :]
+        self.add_vec(0, dq)
+        self.add_vec(1, dv)
+        self.n2[rows, :] += mm_nt(dq, self.w_q[...]) + mm_nt(dk, self.w_k[...]) + mm_nt(dv, self.w_v[...])
+        self.token_copy(i).start()
+
+    def back_task(self, i):
+        pl.when(i < 8)(lambda: self.back_hidden(i))
+        pl.when((i >= 8) & (i < 12))(lambda: self.back_first(i - 8))
+        pl.when((i >= 12) & (i < 36))(lambda: self.attend_back(i - 12))
+        pl.when((i >= 36) & (i < 40))(lambda: self.back_tokens(i - 36))
+
+    def grad_piece(self, i):
+        b = i // 3
+        cols = pl.ds(pl.multiple_of(lax.rem(i, 3) * 256, 256), 256)
+        left = jnp.where(b < 4, G0 + b, jnp.where(b < 8, Y1, jnp.where(b < 9, O, X)))
+        right = jnp.where(b < 4, DZ, jnp.where(b < 8, D0 + b - 4, jnp.where(b < 9, DA, b)))
+        self.ring[lax.rem(b, 2), cols, :] = mm_t(self.acts[left, :, cols], self.acts[right])
+
+
+N_IN = 19
+VECTORS = ("query_bias", "value_bias", "mixer_bias", "first_gain", "first_shift", "shrink_bias", "second_gain",
+           "second_shift")
+
+
+def layer_kernel(*refs):
+    (tokens, lengths, partners, targets, w_q, query_bias, w_k, w_v, value_bias, w_m, mixer_bias, first_gain,
+     first_shift, w_e, expand_bias, w_s, shrink_bias, second_gain, second_shift) = refs[:N_IN]
+    scores, tokens_grad, summed = refs[N_IN:N_IN + 3]
+    rest = refs[N_IN + 3:]
+    (acts, v_q, v_k, v_v, v_m, v_e, v_s, key_row, logs, logs_t, n1, r1, n2, r2, z, n2_sum, every, du, vec, ring,
+     loaded, told, heard, wrote) = rest[:24]
+    first, second = rest[24:24 + N_STREAM_SCRATCH], rest[24 + N_STREAM_SCRATCH:]
     place = Place()
-    first, second = rest[:N_STREAM_SCRATCH], rest[N_STREAM_SCRATCH:]
-
-    def load(b):
-        slot = lax.rem(b, 2)
-        return pltpu.make_async_copy(g_ref.at[b], ring.at[slot], loaded.at[slot])
+    net = Back(
+        acts=acts, w_q=v_q, w_k=v_k, w_v=v_v, w_m=v_m, w_e=v_e, w_s=v_s, query_bias=query_bias, value_bias=value_bias,
+        mixer_bias=mixer_bias, first_gain=first_gain, first_shift=first_shift, expand_bias=expand_bias,
+        shrink_bias=shrink_bias, second_gain=second_gain, second_shift=second_shift, lengths=lengths,
+        partners=partners, targets=targets, scores=scores, tokens_grad=tokens_grad, key_row=key_row, logs=logs,
+        logs_t=logs_t, n1=n1, r1=r1, n2=n2, r2=r2, z=z, n2_sum=n2_sum, every=every, du=du, vec=vec, ring=ring,
+        told=told, heard=heard, wrote=wrote)
+    loads = [pltpu.make_async_copy(src, dst, loaded.at[i]) for i, (src, dst) in enumerate([
+        (tokens, acts.at[X]), (w_q, v_q), (w_k, v_k), (w_v, v_v), (w_m, v_m), (w_e, v_e), (w_s, v_s)])]
+    for copy in loads:
+        copy.start()
 
     def chunk_rows(t, shift):
         t = jnp.clip(t, 0, 36)
@@ -369,50 +676,127 @@
     def out_rows(t, shift):
         return jnp.clip(t, 0, 36) * 256 + shift
 
-    one = Stream(place, 0, 37, first, ring, lambda t: chunk_rows(t, 0), o_ref, lambda t: out_rows(t, 0))
-    two = Stream(place, 1, 36, second, ring, lambda t: chunk_rows(t, 128), o_ref, lambda t: out_rows(t, 128))
+    one = Stream(place, 0, 37, first, ring, lambda t: chunk_rows(t, 0), summed, lambda t: out_rows(t, 0))
+    two = Stream(place, 1, 36, second, ring, lambda t: chunk_rows(t, 128), summed, lambda t: out_rows(t, 128))
     one.prepare()
     two.prepare()
-    greet_neighbours(place)
-    load(jnp.int32(0)).start()
-
-    def step(t, carry):
-        b = t // 3
-
-        @pl.when((lax.rem(t, 3) == 0) & (b < 12))
+    greet_all(place)
+
+    def each(count, task):
+        def step(i, carry):
+            task(i)
+            return carry
+
+        lax.fori_loop(0, count, step, 0)
+
+    net.masks()
+    net.clear()
+    for copy in loads[:4]:
+        copy.wait()
+    each(4, net.project)
+    each(12, net.attend)
+    net.turn_logs()
+    for copy in loads[4:]:
+        copy.wait()
+    each(4, net.feed)
+    await_all()
+    net.gather(place)
+    for s in range(2):
+        net.pair(place, s)
+    net.second_vectors()
+    each(4, net.back_second)
+
+    def step(turn, carry):
+        t = turn - 3
+
+        @pl.when(t >= 0)
         def _():
-            load(b).wait()
-
-        @pl.when(t == 36)
+            @pl.when(t == 36)
+            def _():
+                ring[0, 0:128, :] = jnp.zeros((128, 768), F32)
+                ring[0, 0:16, :] = vec[...]
+
+            for stream in (one, two):
+                stream.wait(t - 1)
+                stream.work(t)
+                stream.start(t)
+
+        pl.when(turn < 36)(lambda: net.grad_piece(turn))
+
+        @pl.when((t >= 0) & (t < 20))
         def _():
-            ring[0, 0:128, :] = s_ref[...]
-
-        for stream in (one, two):
-            stream.wait(t - 1)
-            stream.work(t)
-            stream.start(t)
-
-        @pl.when((lax.rem(t, 3) == 1) & (b + 1 < 12))
-        def _():
-            load(b + 1).start()
+            def run(i, carry):
+                net.back_task(2 * t + i)
+                return carry
+
+            lax.fori_loop(0, 2, run, 0)
 
         return carry
 
-    lax.fori_loop(0, 49, step, 0)
-
-
-def sum_over_all(matrices, vectors):
-    small = jnp.pad(vectors, ((0, 116), (0, 0)))
+    lax.fori_loop(0, 52, step, 0)
+    for i in range(4):
+        net.token_copy(i).wait()
+
+
+def greet_all(place):
+    bar = pltpu.get_barrier_semaphore()
+    chip = place.me // 2
+
+    def hail(k, carry):
+        pl.semaphore_signal(bar, 1, device_id=(lax.rem(chip + k, 16) * 2 + place.c,), device_id_type=MESH)
+        return carry
+
+    pl.semaphore_signal(bar, 1, device_id=(place.sibling,), device_id_type=MESH)
+    lax.fori_loop(1, 16, hail, 0)
+
+
+def await_all():
+    pl.semaphore_wait(pltpu.get_barrier_semaphore(), 16)
+
+
+def whole_layer(*args):
+    anywhere = pl.BlockSpec(memory_space=pl.ANY)
+    vector = pl.BlockSpec(memory_space=pltpu.VMEM)
+    scalars = pl.BlockSpec(memory_space=pltpu.SMEM)
+    specs = [anywhere if a.dtype == BF else vector if a.shape[0] >= 768 else scalars for a in args]
+
+    def low(*shape):
+        return pltpu.VMEM(shape, BF)
+
+    def full(*shape):
+        return pltpu.VMEM(shape, F32)
+
     return pl.pallas_call(
-        sum_kernel,
-        out_shape=jax.ShapeDtypeStruct((37 * 256 - 128, 768), F32),
-        in_specs=[pl.BlockSpec(memory_space=pl.ANY), pl.BlockSpec(memory_space=pltpu.VMEM)],
-        out_specs=pl.BlockSpec(memory_space=pl.ANY),
-        scratch_shapes=[pltpu.VMEM((2, 768, 768), F32), pltpu.SemaphoreType.DMA((2,))]
-        + stream_scratch() + stream_scratch(),
+        layer_kernel,
+        out_shape=(
+            jax.ShapeDtypeStruct((2,), F32),
+            jax.ShapeDtypeStruct((1024, 768), F32),
+            jax.ShapeDtypeStruct((73 * 128, 768), F32),
+        ),
+        in_specs=specs,
+        out_specs=(scalars, anywhere, anywhere),
+        scratch_shapes=[
+            low(N_ACTS, 1024, 768),
+            low(768, 768), low(768, 768), low(768, 768), low(768, 768), low(768, 3072), low(3072, 768),
+            full(2, 8, 512), full(2, 512, 128), full(2, 16, 512),
+            full(1024, 768), full(1024, 128), full(1024, 768), full(1024, 128), full(256, 768), full(2, 8, 768),
+            full(2, 16, 16, 128), full(2, 8, 768), full(16, 768), full(2, 768, 768),
+            pltpu.SemaphoreType.DMA((7,)), pltpu.SemaphoreType.DMA((16,)), pltpu.SemaphoreType.DMA((16,)),
+            pltpu.SemaphoreType.DMA((4,)),
+        ] + stream_scratch() + stream_scratch(),
         compiler_params=pltpu.CompilerParams(
-            collective_id=0, has_side_effects=True, vmem_limit_bytes=48 << 20),
-    )(matrices, small)
+            collective_id=0, has_side_effects=True, vmem_limit_bytes=63 << 20),
+    )(*args)
+
+
+def fused(*args):
+    pair_scores, tokens_grad, summed = whole_layer(*args)
+    blocks = summed[:9216].reshape(12, 768, 768)
+    small = summed[9216:9228]
+    return (
+        pair_scores, tokens_grad, blocks[9], small[0], blocks[10], blocks[11], small[1], blocks[8], small[2],
+        small[3], small[4], jnp.concatenate([blocks[4], blocks[5], blocks[6], blocks[7]], axis=1),
+        small[8:].reshape(3072), summed[:3072], small[5], small[6], small[7])
 
 
 def to_low(value):
@@ -469,7 +853,6 @@
     shrink_bias,
     second_gain,
     second_shift,
-    devices,
 ):
     sents = lengths.shape[0]
     rows_all = tokens.shape[0]
@@ -596,24 +979,23 @@
     tokens_grad = (
         ndot(dquery, query_proj) + ndot(dkey, key_proj) + ndot(dvalue, value_proj) + dfirst
     )
-    if devices == 32 and width == 768 and expand_proj.shape[1] == 4 * width:
-        matrices = jnp.concatenate([
-            shrink_proj_grad.reshape(4, width, width),
-            expand_proj_grad.reshape(width, 4, width).transpose(1, 0, 2),
-            mixer_proj_grad[None], query_proj_grad[None], key_proj_grad[None], value_proj_grad[None]])
-        vectors = jnp.concatenate([
-            query_bias_grad, value_bias_grad, mixer_bias_grad, first_gain_grad, first_shift_grad,
-            shrink_bias_grad, second_gain_grad, second_shift_grad, expand_bias_grad]).reshape(12, width)
-        summed = sum_over_all(matrices, vectors)
-        blocks = summed[:12 * width].reshape(12, width, width)
-        small = summed[12 * width:12 * width + 12]
-        shrink_proj_grad = summed[:4 * width]
-        expand_proj_grad = blocks[4:8].transpose(1, 0, 2).reshape(width, 4 * width)
-        mixer_proj_grad, query_proj_grad, key_proj_grad, value_proj_grad = blocks[8], blocks[9], blocks[10], blocks[11]
-        (query_bias_grad, value_bias_grad, mixer_bias_grad, first_gain_grad, first_shift_grad,
-         shrink_bias_grad, second_gain_grad, second_shift_grad) = [small[i] for i in range(8)]
-        expand_bias_grad = small[8:].reshape(4 * width)
-    else:
+    (
+        query_proj_grad,
+        query_bias_grad,
+        key_proj_grad,
+        value_proj_grad,
+        value_bias_grad,
+        mixer_proj_grad,
+        mixer_bias_grad,
+        first_gain_grad,
+        first_shift_grad,
+        expand_proj_grad,
+        expand_bias_grad,
+        shrink_proj_grad,
+        shrink_bias_grad,
+        second_gain_grad,
+        second_shift_grad,
+    ) = lax.psum(
         (
             query_proj_grad,
             query_bias_grad,
@@ -630,26 +1012,9 @@
             shrink_bias_grad,
             second_gain_grad,
             second_shift_grad,
-        ) = lax.psum(
-            (
-                query_proj_grad,
-                query_bias_grad,
-                key_proj_grad,
-                value_proj_grad,
-                value_bias_grad,
-                mixer_proj_grad,
-                mixer_bias_grad,
-                first_gain_grad,
-                first_shift_grad,
-                expand_proj_grad,
-                expand_bias_grad,
-                shrink_proj_grad,
-                shrink_bias_grad,
-                second_gain_grad,
-                second_shift_grad,
-            ),
-            "dp",
-        )
+        ),
+        "dp",
+    )
     return (
         pair_scores,
         tokens_grad,
@@ -712,6 +1077,7 @@
         P(),
         P(),
     )
+    plain = mesh.shape["dp"] != 32
     return jax.shard_map(
-        partial(per_device, devices=mesh.shape["dp"]), mesh=mesh, in_specs=in_specs, out_specs=out_specs, check_vma=False
-    )
+        per_device if plain else fused, mesh=mesh, in_specs=in_specs, out_specs=out_specs, check_vma=False
+    )

time: 720 us -> 319 us (0.44)
  matrix products: 181 us -> 0 us
  waiting for transfers between devices: 119 us -> 0 us
  local copies, waits for them, and re-layouts: 102 us -> 24.1 us
  Pallas kernels: 214 us -> 290 us
  blocking collectives: 43.7 us -> 0 us
  other arithmetic: 37.8 us -> 4.18 us
  between operations: 15.1 us -> 0.69 us
    dot_general x33 -> x0, matrix products: 181 us -> none  [the longest x6 41.7 us: ndot(): lax.dot_general(left, right, (((1,), (1,)), ((), ())), preferred_element_...]
    unnamed x2 -> x0, waiting for transfers between devices: 119 us -> none
    pallas_call x1, Pallas kernels: 214 us -> 290 us  [whole_layer(): pl.pallas_call(layer_kernel, out_shape=(jax.ShapeDtypeStruct((2,), F32),...]
    all_gather x1 -> x0, blocking collectives: 43.7 us -> none  [per_device(): every = lax.all_gather(pooled, 'dp', axis=0, tiled=True)]
    reshape x8 -> x1, local copies, waits for them, and re-layouts: 28.2 us -> 0.61 us  [fused(): small[8:].reshape(3072)]
    while x39 -> x0, local copies, waits for them, and re-layouts: 20.4 us -> none  [the longest x4 10.3 us: per_device(): lax.map(attend_back, (queries4, keys4, values4, valid, logsum, dmixed))]
    reduce_sum x12 -> x0, other arithmetic: 19.1 us -> none  [the longest x2 5.2 us: attend(): summed = jnp.sum(expd, axis=-1, keepdims=True)]
    unnamed x135 -> x6, local copies, waits for them, and re-layouts: 21.2 us -> 2.18 us
  transfers between devices with their start and end apart: 1 -> 0, of which waited for: 1 -> 0; matrix products, arithmetic and copies ran while one was open for 0% -> 0% of each run, Pallas kernels for 0% -> 0%
where the time goes in v2:
time: 319 us
  Pallas kernels  290 us (91%)
  local copies, waits for them, and re-layouts  24.1 us (8%)
  other arithmetic  4.18 us (1%)
    pallas_call x1, Pallas kernels, whole_layer(): pl.pallas_call(layer_kernel, out_shape=(jax.ShapeDtypeStruct((2,), F32),...  290 us
    slice x1, local copies, waits for them, and re-layouts, fused(): blocks[4]  10.9 us
    slice x1, local copies, waits for them, and re-layouts, fused(): summed[:3072]  8.03 us

profile of v2, /device:TPU:0, one launch (start us, length us, event | category | flops | bytes accessed | tf_op | source)
XLA Modules:
  0.0 318.5 jit_solution(212393728097276840)
XLA Ops:
  0.7 289.5 %shard_map.314 = (f32[2]{0:T(128)}, f32[1024,768]{1,0:T(8,128)}, f32[9344,768]{1,0:T(8,128)}) custom-call(bf16[1024,768]{1,0:T(8,128)(2,1)} %refs_0_.1, s32[2]{0:T(128)} %refs_1_.1, s32[64]{0:T(128)} %refs_2_.1, f32[2]{0:T(128)} %refs_3_.1, bf16[768,768]{1,0:T(8,128)(2,1)} %refs_4_.1, f32[768]{0:T(1024)} %refs_5_.1, bf16[768,768]{1,0:T(8,128)(2,1)} %refs_6_.1, ...), custom_call_target="tpu_custom_call" | custom-call | tf_op jit(solution)/shard_map/pallas_call | solution.py:769
  290.2 0.7 slice.94
  290.9 0.6 reshape.54
  291.5 1.7 slice_reduce_fusion
  293.2 8.0 %slice.95 = f32[3072,768]{1,0:T(8,128)} slice(f32[9344,768]{1,0:T(8,128)} %get-tuple-element.22), slice={[0:3072], [0:768]} | slice | bytes 18874368 | tf_op jit(solution)/shard_map/slice | solution.py:799
  301.3 10.9 %fusion = (f32[768,768]{1,0:T(8,128)S(1)}, f32[768,768]{1,0:T(8,128)S(1)}, f32[768,768]{1,0:T(8,128)}, f32[768,768]{1,0:T(8,128)S(1)}, f32[768,768]{1,0:T(8,128)...) fusion(f32[9344,768]{1,0:T(8,128)} %get-tuple-element.22), kind=kLoop, calls=%fused_computation.9 | loop fusion | bytes 37748736 | tf_op jit(solution)/shard_map/slice | solution.py:798
  312.1 0.0 copy-start.1
  312.1 0.0 copy-start
  312.2 4.2 %pad_maximum_fusion = f32[768,3072]{1,0:T(8,128)} fusion(f32[768,768]{1,0:T(8,128)S(1)} %get-tuple-element.34, f32[768,768]{1,0:T(8,128)S(1)} %get-tuple-element.37, f32[768,768]{1,0:T(8,128)S(1)} %get-tuple-element.32, f32[768,768]{1,0:T(8,128)S(1)} %get-tuple-element.31), kind=kLoop, calls=%fused_computation | loop fusion | flops 7077888 | bytes 18874368 | tf_op jit(solution)/shard_map/concatenate | solution.py:798
  316.3 0.0 copy-done.1
  316.3 0.5 copy.38
  316.8 0.0 copy-done
  316.9 1.7 copy.39
Async XLA Ops:
  312.1 4.2 %copy-start.1 = (f32[2]{0:T(128)S(1)}, f32[2]{0:T(128)}, u32[]{:S(2)}) copy-start(f32[2]{0:T(128)} %get-tuple-element.56) | copy-start | bytes 28
  312.1 4.7 %copy-start = (f32[1024,768]{1,0:T(8,128)S(1)}, f32[1024,768]{1,0:T(8,128)}, u32[]{:S(2)}) copy-start(f32[1024,768]{1,0:T(8,128)} %get-tuple-element.57) | copy-start | bytes 9437188

commit v3 on v2

--- a/solution.py
+++ b/solution.py
@@ -97,12 +97,14 @@
     def copies(self, t):
         place, n = self.place, self.count
         par = t % 2
-        never = t < 0
 
         def remote(i, src, dst, target):
             return pltpu.make_async_remote_copy(
                 src_ref=src, dst_ref=dst, send_sem=self.sent.at[i, par], recv_sem=self.came.at[i, par],
                 device_id=(target,), device_id_type=MESH)
+
+        def tail(i, src, dst, at, size, target):
+            return remote(i, src.at[pl.ds(at, size)], dst.at[par, pl.ds(at, size)], target)
 
         slot, row = self.grad_rows(t)
         other = rows_at(row + 64 * (1 - place.c), 64)
@@ -121,10 +123,14 @@
                     zs.append((copy, when, lead[side] == k, lead[side] == k + 1))
         return [
             (remote(0, self.grad_ref.at[slot, other], self.sib_in.at[par], place.sibling), (t >= 0) & (t < n), True, True),
-            (remote(1, self.a_rs_out, self.a_rs_in.at[par], self.to_a), (t >= 1) & (t < n + 4), True, True),
-            (remote(2, self.a_ag_out, self.a_ag_in.at[par], self.to_a), (t >= 7) & (t < n + 10), True, True),
-            (remote(3, self.b_rs_out, self.b_rs_in.at[par], self.to_b), (t >= 2) & (t < n + 5), True, True),
-            (remote(4, self.b_ag_out, self.b_ag_in.at[par], self.to_b), (t >= 6) & (t < n + 9), True, True),
+            (remote(1, self.a_rs_out, self.a_rs_in.at[par], self.to_a), (t >= 1) & (t < n + 1), True, True),
+            (tail(1, self.a_rs_out, self.a_rs_in, 128, 16, self.to_a), (t >= n + 1) & (t < n + 4), True, True),
+            (tail(2, self.a_ag_out, self.a_ag_in, 128, 16, self.to_a), (t >= 7) & (t < 10), True, True),
+            (remote(2, self.a_ag_out, self.a_ag_in.at[par], self.to_a), (t >= 10) & (t < n + 10), True, True),
+            (remote(3, self.b_rs_out, self.b_rs_in.at[par], self.to_b), (t >= 2) & (t < n + 2), True, True),
+            (tail(3, self.b_rs_out, self.b_rs_in, 64, 8, self.to_b), (t >= n + 2) & (t < n + 5), True, True),
+            (tail(4, self.b_ag_out, self.b_ag_in, 64, 8, self.to_b), (t >= 6) & (t < 9), True, True),
+            (remote(4, self.b_ag_out, self.b_ag_in.at[par], self.to_b), (t >= 9) & (t < n + 9), True, True),
             (remote(9, self.full.at[ring], self.out_ref.at[mine], place.sibling), (t >= 11) & (t < n + 11), True, True),
         ] + zs, (pltpu.make_async_copy(self.full.at[ring], self.out_ref.at[mine], self.kept.at[par]), (t >= 11) & (t < n + 11))
 
@@ -360,20 +366,13 @@
 
 
 def normal_cdf(pre):
-    size = jnp.abs(pre)
-    down = 1.0 + (0.3275911 / 1.4142135623730951) * size
-    t = pl.reciprocal(down, approx=True)
-    t = t * (2.0 - down * t)
-    bell = jnp.exp(-0.5 * pre * pre)
-    poly = t * (0.5 * 0.254829592 + t * (0.5 * -0.284496736 + t * (0.5 * 1.421413741 + t * (
-        0.5 * -1.453152027 + t * (0.5 * 1.061405429)))))
-    tail = poly * bell
-    return jnp.where(pre >= 0, 1.0 - tail, tail), bell
+    return 0.5 + 0.5 * lax.erf(pre * 0.7071067811865476), jnp.exp(-0.5 * pre * pre)
 
 
 G0, D0 = 0, 4
 X, Q, K, V, O, Y1, DZ, DA, DO = 8, 9, 10, 11, 12, 13, 14, 15, 16
 N_ACTS = 17
+ROWS = 512
 
 
 class Net:
@@ -381,7 +380,7 @@
         self.__dict__.update(refs)
 
     def project(self, i):
-        rows = pl.ds(pl.multiple_of(i * 256, 256), 256)
+        rows = pl.ds(pl.multiple_of(i * ROWS, ROWS), ROWS)
         acts = self.acts
         x = acts[X, rows, :]
         acts[Q, rows, :] = (mm(x, self.w_q[...]) + row_of(self.query_bias)).astype(BF) * BF(0.125)
@@ -402,26 +401,21 @@
         v = acts[V, rows, lanes]
         lane = lax.broadcasted_iota(jnp.int32, (1, 128), 1)
         v_ones = jnp.concatenate([v, jnp.ones((512, 128), BF)], axis=1)
-        step = 256
-        for part in range(512 // step):
-            some = pl.ds(pl.multiple_of(s * 512 + part * step, step), step)
-            q = acts[Q, some, lanes]
-            outs = []
-            tops = []
-            for head in range(2):
-                live = (lane >= 64) if head else (lane < 64)
-                score = mm_nt(jnp.where(live, q, BF(0)), k) + self.key_row[s, 0:1, :]
-                top = jnp.max(score, axis=1, keepdims=True)
-                e = jnp.exp(score - top).astype(BF)
-                both = mm(e, v_ones)
-                total = both[:, 128:]
-                outs.append(both[:, :128] / total)
-                tops.append(top + jnp.log(total))
-            acts[O, some, lanes] = jnp.where(lane < 64, outs[0], outs[1]).astype(BF)
-            spot = pl.ds(part * step, step)
-            old = self.logs[s, spot, :]
-            old = jnp.where(lane == 2 * pair, tops[0], old)
-            self.logs[s, spot, :] = jnp.where(lane == 2 * pair + 1, tops[1], old)
+        q = acts[Q, rows, lanes]
+        boths, tops = [], []
+        for head in range(2):
+            live = (lane >= 64) if head else (lane < 64)
+            score = mm_nt(jnp.where(live, q, BF(0)), k) + self.key_row[s, 0:1, :]
+            top = jnp.max(score, axis=1, keepdims=True)
+            boths.append(mm(jnp.exp(score - top).astype(BF), v_ones))
+            tops.append(top)
+        pick = lane < 64
+        mixed = jnp.where(pick, boths[0][:, :128], boths[1][:, :128])
+        total = jnp.where(pick, boths[0][:, 128:], boths[1][:, 128:])
+        acts[O, rows, lanes] = (mixed * pl.reciprocal(total, approx=False)).astype(BF)
+        one, two = lane == 2 * pair, lane == 2 * pair + 1
+        self.logs[s] = jnp.where(one, tops[0], jnp.where(two, tops[1], self.logs[s]))
+        self.sums[s] = jnp.where(one, boths[0][:, 128:], jnp.where(two, boths[1][:, 128:], self.sums[s]))
 
     def normed(self, rows):
         mean = jnp.sum(rows, axis=1, keepdims=True) * (1.0 / 768)
@@ -431,12 +425,12 @@
         return centred * inverse, inverse
 
     def feed(self, i):
-        rows = pl.ds(pl.multiple_of(i * 256, 256), 256)
+        rows = pl.ds(pl.multiple_of(i * ROWS, ROWS), ROWS)
         acts = self.acts
         h1 = acts[X, rows, :].astype(F32) + mm(acts[O, rows, :], self.w_m[...]) + row_of(self.mixer_bias)
         n1, r1 = self.normed(h1)
         self.n1[rows, :] = n1.astype(self.n1.dtype)
-        self.r1[rows, :] = jnp.broadcast_to(r1, (256, 128))
+        self.r1[rows, :] = jnp.broadcast_to(r1, (ROWS, 128))
         y1 = n1 * row_of(self.first_gain) + row_of(self.first_shift)
         self.z[...] = y1 + row_of(self.shrink_bias)
         acts[Y1, rows, :] = y1.astype(BF)
@@ -444,13 +438,13 @@
             self.feed_block(rows, j)
         n2, r2 = self.normed(self.z[...])
         self.n2[rows, :] = n2
-        self.r2[rows, :] = jnp.broadcast_to(r2, (256, 128))
-        s = i // 2
-        at = lax.broadcasted_iota(jnp.int32, (256, 1), 0) + lax.rem(i, 2) * 256
+        self.r2[rows, :] = jnp.broadcast_to(r2, (ROWS, 128))
+        each = 512 // ROWS
+        s, part = i // each, lax.rem(i, each)
+        at = lax.broadcasted_iota(jnp.int32, (ROWS, 1), 0) + part * ROWS
         live = jnp.where(at < self.lengths[s], n2, 0.0)
-        part = jnp.sum(live, axis=0, keepdims=True)
-        first = lax.rem(i, 2) == 0
-        self.n2_sum[s, 0:1, :] = jnp.where(first, part, self.n2_sum[s, 0:1, :] + part)
+        some = jnp.sum(live, axis=0, keepdims=True)
+        self.n2_sum[s, 0:1, :] = jnp.where(part == 0, some, self.n2_sum[s, 0:1, :] + some)
 
     def feed_block(self, rows, j):
         acts = self.acts
@@ -470,7 +464,7 @@
 class Back(Net):
     def turn_logs(self):
         for s in range(2):
-            self.logs_t[s] = jnp.transpose(self.logs[s])[0:16, :]
+            self.logs_t[s] = jnp.transpose(self.logs[s] + jnp.log(self.sums[s]))[0:16, :]
 
     def gather(self, place):
         c, chip = place.c, place.me // 2
@@ -486,21 +480,17 @@
                 src_ref=every.at[c, source], dst_ref=every.at[c, source], send_sem=self.told.at[device // 2],
                 recv_sem=self.heard.at[source], device_id=(device,), device_id_type=MESH)
 
-        def out(k, carry):
+        order = (12, 4, 13, 11, 3, 5, 14, 10, 2, 6, 15, 9, 1, 7, 8)
+        for k in order:
             copy(chip, lax.rem(chip + k, 16) * 2 + c).start()
-            return carry
-
-        def done(k, carry):
-            copy(chip, lax.rem(chip + k, 16) * 2 + c).wait_send()
+        for k in order:
             copy(lax.rem(chip + 16 - k, 16), place.me).wait_recv()
-            return carry
-
-        lax.fori_loop(1, 16, out, 0)
-        lax.fori_loop(1, 16, done, 0)
         share = pltpu.make_async_remote_copy(
             src_ref=every.at[c], dst_ref=every.at[c], send_sem=self.told.at[chip],
             recv_sem=self.heard.at[chip], device_id=(place.sibling,), device_id_type=MESH)
         share.start()
+        for k in order:
+            copy(chip, lax.rem(chip + k, 16) * 2 + c).wait_send()
         share.wait_send()
         share.wait_recv()
 
@@ -518,7 +508,7 @@
             return far, near
 
         nothing = jnp.zeros((8, 128), F32)
-        far, near = lax.fori_loop(0, 64, pick, (nothing, nothing))
+        far, near = lax.fori_loop(0, 64, pick, (nothing, nothing), unroll=8)
         live = lax.broadcasted_iota(jnp.int32, (8, 128), 0) < 6
 
         def inner(left, right):
@@ -540,6 +530,8 @@
 
     def clear(self):
         self.vec[...] = jnp.zeros_like(self.vec)
+        self.logs[...] = jnp.zeros_like(self.logs)
+        self.sums[...] = jnp.ones_like(self.sums)
 
     def add_vec(self, at, rows):
         self.vec[at:at + 1, :] += jnp.sum(rows.astype(F32), axis=0, keepdims=True)
@@ -637,10 +629,11 @@
 
     def grad_piece(self, i):
         b = i // 3
+        slot = lax.rem(i, 2)
         cols = pl.ds(pl.multiple_of(lax.rem(i, 3) * 256, 256), 256)
         left = jnp.where(b < 4, G0 + b, jnp.where(b < 8, Y1, jnp.where(b < 9, O, X)))
         right = jnp.where(b < 4, DZ, jnp.where(b < 8, D0 + b - 4, jnp.where(b < 9, DA, b)))
-        self.ring[lax.rem(b, 2), cols, :] = mm_t(self.acts[left, :, cols], self.acts[right])
+        self.ring[slot] = mm_t(self.acts[left, :, cols], self.acts[right])
 
 
 N_IN = 19
@@ -653,25 +646,25 @@
      first_shift, w_e, expand_bias, w_s, shrink_bias, second_gain, second_shift) = refs[:N_IN]
     scores, tokens_grad, summed = refs[N_IN:N_IN + 3]
     rest = refs[N_IN + 3:]
-    (acts, v_q, v_k, v_v, v_m, v_e, v_s, key_row, logs, logs_t, n1, r1, n2, r2, z, n2_sum, every, du, vec, ring,
-     loaded, told, heard, wrote) = rest[:24]
-    first, second = rest[24:24 + N_STREAM_SCRATCH], rest[24 + N_STREAM_SCRATCH:]
+    (acts, v_q, v_k, v_v, v_m, v_e, v_s, key_row, logs, sums, logs_t, n1, r1, n2, r2, z, n2_sum, every, du, vec, ring,
+     loaded, told, heard, wrote) = rest[:25]
+    first, second = rest[25:25 + N_STREAM_SCRATCH], rest[25 + N_STREAM_SCRATCH:]
     place = Place()
     net = Back(
         acts=acts, w_q=v_q, w_k=v_k, w_v=v_v, w_m=v_m, w_e=v_e, w_s=v_s, query_bias=query_bias, value_bias=value_bias,
         mixer_bias=mixer_bias, first_gain=first_gain, first_shift=first_shift, expand_bias=expand_bias,
         shrink_bias=shrink_bias, second_gain=second_gain, second_shift=second_shift, lengths=lengths,
-        partners=partners, targets=targets, scores=scores, tokens_grad=tokens_grad, key_row=key_row, logs=logs,
+        partners=partners, targets=targets, scores=scores, tokens_grad=tokens_grad, key_row=key_row, logs=logs, sums=sums,
         logs_t=logs_t, n1=n1, r1=r1, n2=n2, r2=r2, z=z, n2_sum=n2_sum, every=every, du=du, vec=vec, ring=ring,
         told=told, heard=heard, wrote=wrote)
     loads = [pltpu.make_async_copy(src, dst, loaded.at[i]) for i, (src, dst) in enumerate([
         (tokens, acts.at[X]), (w_q, v_q), (w_k, v_k), (w_v, v_v), (w_m, v_m), (w_e, v_e), (w_s, v_s)])]
-    for copy in loads:
+    for copy in loads[:4]:
         copy.start()
 
     def chunk_rows(t, shift):
         t = jnp.clip(t, 0, 36)
-        return lax.rem(t // 3, 2), lax.rem(t, 3) * 256 + shift
+        return lax.rem(t, 2), shift
 
     def out_rows(t, shift):
         return jnp.clip(t, 0, 36) * 256 + shift
@@ -693,12 +686,14 @@
     net.clear()
     for copy in loads[:4]:
         copy.wait()
-    each(4, net.project)
+    for copy in loads[4:]:
+        copy.start()
+    each(1024 // ROWS, net.project)
     each(12, net.attend)
     net.turn_logs()
     for copy in loads[4:]:
         copy.wait()
-    each(4, net.feed)
+    each(1024 // ROWS, net.feed)
     await_all()
     net.gather(place)
     for s in range(2):
@@ -706,34 +701,30 @@
     net.second_vectors()
     each(4, net.back_second)
 
+    first_task = 12
+
     def step(turn, carry):
-        t = turn - 3
-
-        @pl.when(t >= 0)
+        t = turn // 2 - 1
+        side = lax.rem(turn, 2)
+
+        @pl.when(turn == 74)
         def _():
-            @pl.when(t == 36)
-            def _():
-                ring[0, 0:128, :] = jnp.zeros((128, 768), F32)
-                ring[0, 0:16, :] = vec[...]
-
-            for stream in (one, two):
+            ring[0, 0:128, :] = jnp.zeros((128, 768), F32)
+            ring[0, 0:16, :] = vec[...]
+
+        for i, stream in enumerate((one, two)):
+            @pl.when((side == i) & (t >= 0))
+            def _(stream=stream):
                 stream.wait(t - 1)
                 stream.work(t)
                 stream.start(t)
 
-        pl.when(turn < 36)(lambda: net.grad_piece(turn))
-
-        @pl.when((t >= 0) & (t < 20))
-        def _():
-            def run(i, carry):
-                net.back_task(2 * t + i)
-                return carry
-
-            lax.fori_loop(0, 2, run, 0)
-
+        pl.when((side == 1) & (t + 1 < 36))(lambda: net.grad_piece(t + 1))
+        task = turn - 2 - first_task
+        pl.when((task >= 0) & (task < 40))(lambda: net.back_task(task))
         return carry
 
-    lax.fori_loop(0, 52, step, 0)
+    lax.fori_loop(1, 2 * 49 + 2, step, 0)
     for i in range(4):
         net.token_copy(i).wait()
 
@@ -778,9 +769,9 @@
         scratch_shapes=[
             low(N_ACTS, 1024, 768),
             low(768, 768), low(768, 768), low(768, 768), low(768, 768), low(768, 3072), low(3072, 768),
-            full(2, 8, 512), full(2, 512, 128), full(2, 16, 512),
-            full(1024, 768), full(1024, 128), full(1024, 768), full(1024, 128), full(256, 768), full(2, 8, 768),
-            full(2, 16, 16, 128), full(2, 8, 768), full(16, 768), full(2, 768, 768),
+            full(2, 8, 512), full(2, 512, 128), full(2, 512, 128), full(2, 16, 512),
+            full(1024, 768), full(1024, 128), full(1024, 768), full(1024, 128), full(ROWS, 768), full(2, 8, 768),
+            full(2, 16, 16, 128), full(2, 8, 768), full(16, 768), full(2, 256, 768),
             pltpu.SemaphoreType.DMA((7,)), pltpu.SemaphoreType.DMA((16,)), pltpu.SemaphoreType.DMA((16,)),
             pltpu.SemaphoreType.DMA((4,)),
         ] + stream_scratch() + stream_scratch(),
@@ -789,14 +780,75 @@
     )(*args)
 
 
+def deliver_kernel(count, height, summed, tokens_sum, scores, *refs):
+    (scores_out, tokens_out, w_q, query_bias, w_k, w_v, value_bias, w_m, mixer_bias, first_gain, first_shift, w_e,
+     expand_bias, w_s, shrink_bias, second_gain, second_shift) = refs[:17]
+    buffer, small, came, left, small_came = refs[17:]
+    jobs = []
+    for row in range(0, 3072, height):
+        jobs.append((summed.at[pl.ds(row, height)], w_s.at[pl.ds(row, height)]))
+    for row in range(0, 3072, height):
+        block, at = row // 768, row % 768
+        jobs.append((summed.at[pl.ds(3072 + row, height)], w_e.at[pl.ds(at, height), pl.ds(768 * block, 768)]))
+    for row in range(0, 3072, height):
+        block, at = row // 768, row % 768
+        jobs.append((summed.at[pl.ds(6144 + row, height)], (w_m, w_q, w_k, w_v)[block].at[pl.ds(at, height)]))
+    rows = tokens_sum.shape[0]
+    for row in range(0, rows, height):
+        size = min(height, rows - row)
+        jobs.append((tokens_sum.at[pl.ds(row, size)], tokens_out.at[pl.ds(row, size)]))
+
+    def copies(i):
+        src, dst = jobs[i]
+        spot = buffer.at[i % count, pl.ds(0, src.shape[0])]
+        return (pltpu.make_async_copy(src, spot, came.at[i % count]),
+                pltpu.make_async_copy(spot, dst, left.at[i % count]))
+
+    total = len(jobs)
+    ahead = count // 2
+    vectors = pltpu.make_async_copy(summed.at[pl.ds(9216, 16)], small, small_came)
+    vectors.start()
+    for i in range(min(ahead, total)):
+        copies(i)[0].start()
+    for i in range(total):
+        copies(i)[0].wait()
+        copies(i)[1].start()
+        later = i + ahead
+        if later < total:
+            if later >= count:
+                copies(later - count)[1].wait()
+            copies(later)[0].start()
+        if i == 0:
+            vectors.wait()
+            for j, ref in enumerate((query_bias, value_bias, mixer_bias, first_gain, first_shift, shrink_bias,
+                                     second_gain, second_shift)):
+                ref[...] = small[j, :]
+            for j in range(4):
+                expand_bias[768 * j:768 * j + 768] = small[8 + j, :]
+            for s in range(2):
+                scores_out[s] = scores[s]
+    for i in range(max(0, total - count), total):
+        copies(i)[1].wait()
+
+
 def fused(*args):
     pair_scores, tokens_grad, summed = whole_layer(*args)
-    blocks = summed[:9216].reshape(12, 768, 768)
-    small = summed[9216:9228]
-    return (
-        pair_scores, tokens_grad, blocks[9], small[0], blocks[10], blocks[11], small[1], blocks[8], small[2],
-        small[3], small[4], jnp.concatenate([blocks[4], blocks[5], blocks[6], blocks[7]], axis=1),
-        small[8:].reshape(3072), summed[:3072], small[5], small[6], small[7])
+    anywhere = pl.BlockSpec(memory_space=pl.ANY)
+    vector = pl.BlockSpec(memory_space=pltpu.VMEM)
+    scalars = pl.BlockSpec(memory_space=pltpu.SMEM)
+    shapes = [(2,), (1024, 768), (768, 768), (768,), (768, 768), (768, 768), (768,), (768, 768), (768,), (768,), (768,),
+              (768, 3072), (3072,), (3072, 768), (768,), (768,), (768,)]
+    count, height = 16, 384
+    return tuple(pl.pallas_call(
+        partial(deliver_kernel, count, height),
+        out_shape=[jax.ShapeDtypeStruct(shape, F32) for shape in shapes],
+        in_specs=[anywhere, pl.BlockSpec(memory_space=pltpu.HBM), scalars],
+        out_specs=[anywhere if len(shape) == 2 else vector if shape[0] > 2 else scalars for shape in shapes],
+        scratch_shapes=[pltpu.VMEM((count, height, 768), F32), pltpu.VMEM((16, 768), F32),
+                        pltpu.SemaphoreType.DMA((count,)), pltpu.SemaphoreType.DMA((count,)),
+                        pltpu.SemaphoreType.DMA],
+        compiler_params=pltpu.CompilerParams(vmem_limit_bytes=60 << 20),
+    )(summed, tokens_grad, pair_scores))
 
 
 def to_low(value):

time: 319 us -> 286 us (0.90)
  local copies, waits for them, and re-layouts: 24.1 us -> 0 us
  Pallas kernels: 290 us -> 285 us
  other arithmetic: 4.18 us -> 0 us
    pallas_call x1, Pallas kernels: 290 us -> 262 us  [whole_layer(): pl.pallas_call(layer_kernel, out_shape=(jax.ShapeDtypeStruct((2,), F32),...]
    pallas_call x0 -> x1, Pallas kernels: none -> 22.9 us  [fused(): pl.pallas_call(partial(deliver_kernel, count, height), out_shape=[jax.Sha...]
    slice x4 -> x0, local copies, waits for them, and re-layouts: 21.3 us -> none  [the longest x1 10.9 us: fused(): blocks[4]]
    concatenate x1 -> x0, other arithmetic: 4.18 us -> none  [fused(): jnp.concatenate([blocks[4], blocks[5], blocks[6], blocks[7]], axis=1)]
where the time goes in v3:
time: 286 us
  Pallas kernels  285 us (100%)
    pallas_call x1, Pallas kernels, whole_layer(): pl.pallas_call(layer_kernel, out_shape=(jax.ShapeDtypeStruct((2,), F32),...  262 us
    pallas_call x1, Pallas kernels, fused(): pl.pallas_call(partial(deliver_kernel, count, height), out_shape=[jax.Sha...  22.9 us

profile of v3, /device:TPU:0, one launch (start us, length us, event | category | flops | bytes accessed | tf_op | source)
XLA Modules:
  0.0 285.8 jit_solution(13577550574031900527)
XLA Ops:
  0.7 262.0 %shard_map.314 = (f32[2]{0:T(128)}, f32[1024,768]{1,0:T(8,128)}, f32[9344,768]{1,0:T(8,128)}) custom-call(bf16[1024,768]{1,0:T(8,128)(2,1)} %refs_0_.1, s32[2]{0:T(128)} %refs_1_.1, s32[64]{0:T(128)} %refs_2_.1, f32[2]{0:T(128)} %refs_3_.1, bf16[768,768]{1,0:T(8,128)(2,1)} %refs_4_.1, f32[768]{0:T(1024)} %refs_5_.1, bf16[768,768]{1,0:T(8,128)(2,1)} %refs_6_.1, ...), custom_call_target="tpu_custom_call" | custom-call | tf_op jit(solution)/shard_map/pallas_call | solution.py:760
  262.7 22.9 %shard_map.315 = (f32[2]{0:T(128)}, f32[1024,768]{1,0:T(8,128)}, f32[768,768]{1,0:T(8,128)}, f32[768]{0:T(1024)}, f32[768,768]{1,0:T(8,128)}, /*index=5*/f32[768...) custom-call(f32[9344,768]{1,0:T(8,128)} %get-tuple-element.20.summed, ...), custom_call_target="tpu_custom_call" | custom-call | tf_op jit(solution)/shard_map/pallas_call | solution.py:842

commit v4 on v3

--- a/solution.py
+++ b/solution.py
@@ -73,7 +73,7 @@
 
 
 class Stream:
-    def __init__(self, place, which, count, refs, grad_ref, grad_rows, out_ref, out_rows):
+    def __init__(self, place, which, count, refs, grad_ref, grad_rows, outs):
         (self.sib_in, self.a_rs_out, self.a_rs_in, self.a_ag_out, self.a_ag_in, self.b_rs_out, self.b_rs_in,
          self.b_ag_out, self.b_ag_in, self.z_out, self.z_in, self.p1, self.p2, self.p3, self.q1, self.q2, self.q3,
          self.full, self.sent, self.came, self.kept) = refs
@@ -81,8 +81,7 @@
         self.count = count
         self.grad_ref = grad_ref
         self.grad_rows = grad_rows
-        self.out_ref = out_ref
-        self.out_rows = out_rows
+        self.outs = outs
         if which == 0:
             self.d1, self.d2, self.to_a, self.to_b = place.x, place.y, place.to_x, place.to_y
         else:
@@ -110,8 +109,7 @@
         other = rows_at(row + 64 * (1 - place.c), 64)
         m = t - 11
         ring = lax.rem(t + 5, 8)
-        out_row = self.out_rows(m)
-        mine = rows_at(out_row + 64 * place.c, 64)
+        outs = self.outs(m, 64 * place.c)
         lead = (place.z, 3 - place.z)
         zs = []
         for side, device in ((0, place.up), (1, place.down)):
@@ -131,17 +129,21 @@
             (tail(3, self.b_rs_out, self.b_rs_in, 64, 8, self.to_b), (t >= n + 2) & (t < n + 5), True, True),
             (tail(4, self.b_ag_out, self.b_ag_in, 64, 8, self.to_b), (t >= 6) & (t < 9), True, True),
             (remote(4, self.b_ag_out, self.b_ag_in.at[par], self.to_b), (t >= 9) & (t < n + 9), True, True),
-            (remote(9, self.full.at[ring], self.out_ref.at[mine], place.sibling), (t >= 11) & (t < n + 11), True, True),
-        ] + zs, (pltpu.make_async_copy(self.full.at[ring], self.out_ref.at[mine], self.kept.at[par]), (t >= 11) & (t < n + 11))
+        ] + zs + [
+            (remote(9, self.full.at[ring], spot, place.sibling), (t >= 11) & (t < n + 11) & when, True, True)
+            for spot, when in outs
+        ], [(pltpu.make_async_copy(self.full.at[ring], spot, self.kept.at[par]), (t >= 11) & (t < n + 11) & when)
+            for spot, when in outs]
 
     def start(self, t):
-        remote, (local, live) = self.copies(t)
+        remote, local = self.copies(t)
         for copy, when, sends, _ in remote:
             pl.when(when if sends is True else when & sends)(copy.start)
-        pl.when(live)(local.start)
+        for copy, when in local:
+            pl.when(when)(copy.start)
 
     def wait(self, t):
-        remote, (local, live) = self.copies(t)
+        remote, local = self.copies(t)
         for copy, when, sends, takes in remote:
             if sends is True:
                 @pl.when(when)
@@ -151,7 +153,8 @@
             else:
                 pl.when(when & sends)(copy.wait_send)
                 pl.when(when & takes)(copy.wait_recv)
-        pl.when(live)(local.wait)
+        for copy, when in local:
+            pl.when(when)(copy.wait)
 
     def work(self, t):
         place = self.place
@@ -373,19 +376,25 @@
 X, Q, K, V, O, Y1, DZ, DA, DO = 8, 9, 10, 11, 12, 13, 14, 15, 16
 N_ACTS = 17
 ROWS = 512
+LATE = 8
 
 
 class Net:
     def __init__(self, **refs):
         self.__dict__.update(refs)
 
-    def project(self, i):
+    def project_q(self, i):
         rows = pl.ds(pl.multiple_of(i * ROWS, ROWS), ROWS)
-        acts = self.acts
-        x = acts[X, rows, :]
-        acts[Q, rows, :] = (mm(x, self.w_q[...]) + row_of(self.query_bias)).astype(BF) * BF(0.125)
-        acts[K, rows, :] = mm(x, self.w_k[...]).astype(BF)
-        acts[V, rows, :] = (mm(x, self.w_v[...]) + row_of(self.value_bias)).astype(BF)
+        out = mm(self.acts[X, rows, :], self.w_q[...]) + row_of(self.query_bias)
+        self.acts[Q, rows, :] = out.astype(BF) * BF(0.125)
+
+    def project_k(self, i):
+        rows = pl.ds(pl.multiple_of(i * ROWS, ROWS), ROWS)
+        self.acts[K, rows, :] = mm(self.acts[X, rows, :], self.w_k[...]).astype(BF)
+
+    def project_v(self, i):
+        rows = pl.ds(pl.multiple_of(i * ROWS, ROWS), ROWS)
+        self.acts[V, rows, :] = (mm(self.acts[X, rows, :], self.w_v[...]) + row_of(self.value_bias)).astype(BF)
 
     def masks(self):
         place = lax.broadcasted_iota(jnp.int32, (8, 512), 1)
@@ -462,6 +471,32 @@
 
 
 class Back(Net):
+    def share_vectors(self, place, k):
+        mine = rows_at(8 * place.c, 8)
+        z = place.z
+        target = (place.sibling, place.to_x, place.to_y, place.me + 8 - 16 * (z % 2), place.me + 16 - 32 * (z // 2),
+                  place.sibling)[k]
+        source = self.vec.at[rows_at(8 * (1 - place.c), 8)] if k == 0 else self.vec.at[mine]
+        landing = self.vec.at[mine] if k == 5 else self.vec_in.at[k]
+        return pltpu.make_async_remote_copy(
+            src_ref=source, dst_ref=landing, send_sem=self.vec_sent.at[k], recv_sem=self.vec_came.at[k],
+            device_id=(target,), device_id_type=MESH)
+
+    def sum_vectors(self, place, turn):
+        mine = rows_at(8 * place.c, 8)
+        for k in range(6):
+            @pl.when(turn == 76 + 3 * k)
+            def _(k=k):
+                self.share_vectors(place, k).start()
+
+            @pl.when(turn == 79 + 3 * k)
+            def _(k=k):
+                copy = self.share_vectors(place, k)
+                copy.wait_send()
+                copy.wait_recv()
+                if k < 5:
+                    self.vec[mine, :] += self.vec_in[k]
+
     def turn_logs(self):
         for s in range(2):
             self.logs_t[s] = jnp.transpose(self.logs[s] + jnp.log(self.sums[s]))[0:16, :]
@@ -526,7 +561,7 @@
         grad += near_miss * (near / (near_length * length) - near_score * own)
         for j in range(6):
             self.du[s, 0:1, 128 * j:128 * j + 128] = grad[j:j + 1, :]
-        self.scores[s] = jnp.sum(score)
+        self.scores[s:s + 1, :] = jnp.broadcast_to(score, (1, 128))
 
     def clear(self):
         self.vec[...] = jnp.zeros_like(self.vec)
@@ -609,17 +644,12 @@
         acts[K, rows, lanes] = jnp.where(live, dk.astype(BF), k)
         acts[V, rows, lanes] = jnp.where(live, dv.astype(BF), v)
 
-    def token_copy(self, i):
-        rows = pl.ds(pl.multiple_of(i * 256, 256), 256)
-        return pltpu.make_async_copy(self.n2.at[rows], self.tokens_grad.at[rows], self.wrote.at[i])
-
     def back_tokens(self, i):
         rows = pl.ds(pl.multiple_of(i * 256, 256), 256)
         dq, dk, dv = self.acts[Q, rows, :], self.acts[K, rows, :], self.acts[V, rows, :]
         self.add_vec(0, dq)
         self.add_vec(1, dv)
         self.n2[rows, :] += mm_nt(dq, self.w_q[...]) + mm_nt(dk, self.w_k[...]) + mm_nt(dv, self.w_v[...])
-        self.token_copy(i).start()
 
     def back_task(self, i):
         pl.when(i < 8)(lambda: self.back_hidden(i))
@@ -637,6 +667,7 @@
 
 
 N_IN = 19
+VMEM_LIMIT = 54 << 20
 VECTORS = ("query_bias", "value_bias", "mixer_bias", "first_gain", "first_shift", "shrink_bias", "second_gain",
            "second_shift")
 
@@ -644,19 +675,20 @@
 def layer_kernel(*refs):
     (tokens, lengths, partners, targets, w_q, query_bias, w_k, w_v, value_bias, w_m, mixer_bias, first_gain,
      first_shift, w_e, expand_bias, w_s, shrink_bias, second_gain, second_shift) = refs[:N_IN]
-    scores, tokens_grad, summed = refs[N_IN:N_IN + 3]
-    rest = refs[N_IN + 3:]
-    (acts, v_q, v_k, v_v, v_m, v_e, v_s, key_row, logs, sums, logs_t, n1, r1, n2, r2, z, n2_sum, every, du, vec, ring,
-     loaded, told, heard, wrote) = rest[:25]
-    first, second = rest[25:25 + N_STREAM_SCRATCH], rest[25 + N_STREAM_SCRATCH:]
+    scores, late, vec, summed = refs[N_IN:N_IN + 4]
+    rest = refs[N_IN + 4:]
+    (acts, v_q, v_k, v_v, v_m, v_e, v_s, key_row, logs, sums, logs_t, r1, r2, n2_sum, every, du, vec_in, ring,
+     loaded, told, heard, vec_sent, vec_came) = rest[:23]
+    n2, n1, z = late.at[pl.ds(0, 1024)], late.at[pl.ds(1024, 1024)], late.at[pl.ds(2048, ROWS)]
+    first, second = rest[23:23 + N_STREAM_SCRATCH], rest[23 + N_STREAM_SCRATCH:]
     place = Place()
     net = Back(
         acts=acts, w_q=v_q, w_k=v_k, w_v=v_v, w_m=v_m, w_e=v_e, w_s=v_s, query_bias=query_bias, value_bias=value_bias,
         mixer_bias=mixer_bias, first_gain=first_gain, first_shift=first_shift, expand_bias=expand_bias,
         shrink_bias=shrink_bias, second_gain=second_gain, second_shift=second_shift, lengths=lengths,
-        partners=partners, targets=targets, scores=scores, tokens_grad=tokens_grad, key_row=key_row, logs=logs, sums=sums,
+        partners=partners, targets=targets, scores=scores, key_row=key_row, logs=logs, sums=sums,
         logs_t=logs_t, n1=n1, r1=r1, n2=n2, r2=r2, z=z, n2_sum=n2_sum, every=every, du=du, vec=vec, ring=ring,
-        told=told, heard=heard, wrote=wrote)
+        told=told, heard=heard, vec_in=vec_in, vec_sent=vec_sent, vec_came=vec_came)
     loads = [pltpu.make_async_copy(src, dst, loaded.at[i]) for i, (src, dst) in enumerate([
         (tokens, acts.at[X]), (w_q, v_q), (w_k, v_k), (w_v, v_v), (w_m, v_m), (w_e, v_e), (w_s, v_s)])]
     for copy in loads[:4]:
@@ -666,11 +698,13 @@
         t = jnp.clip(t, 0, 36)
         return lax.rem(t, 2), shift
 
-    def out_rows(t, shift):
-        return jnp.clip(t, 0, 36) * 256 + shift
-
-    one = Stream(place, 0, 37, first, ring, lambda t: chunk_rows(t, 0), summed, lambda t: out_rows(t, 0))
-    two = Stream(place, 1, 36, second, ring, lambda t: chunk_rows(t, 128), summed, lambda t: out_rows(t, 128))
+    def outs(m, shift):
+        early = rows_at(jnp.clip(m, 0, 35 - LATE) * 256 + shift, 64)
+        last = rows_at(1024 + (jnp.clip(m, 36 - LATE, 35) - (36 - LATE)) * 256 + shift, 64)
+        return [(summed.at[early], m < 36 - LATE), (late.at[last], m >= 36 - LATE)]
+
+    one = Stream(place, 0, 36, first, ring, lambda t: chunk_rows(t, 0), outs)
+    two = Stream(place, 1, 36, second, ring, lambda t: chunk_rows(t, 128), lambda m, at: outs(m, 128 + at))
     one.prepare()
     two.prepare()
     greet_all(place)
@@ -684,11 +718,15 @@
 
     net.masks()
     net.clear()
-    for copy in loads[:4]:
-        copy.wait()
+    loads[0].wait()
+    loads[1].wait()
+    each(1024 // ROWS, net.project_q)
+    loads[2].wait()
+    loads[3].wait()
     for copy in loads[4:]:
         copy.start()
-    each(1024 // ROWS, net.project)
+    each(1024 // ROWS, net.project_k)
+    each(1024 // ROWS, net.project_v)
     each(12, net.attend)
     net.turn_logs()
     for copy in loads[4:]:
@@ -707,11 +745,6 @@
         t = turn // 2 - 1
         side = lax.rem(turn, 2)
 
-        @pl.when(turn == 74)
-        def _():
-            ring[0, 0:128, :] = jnp.zeros((128, 768), F32)
-            ring[0, 0:16, :] = vec[...]
-
         for i, stream in enumerate((one, two)):
             @pl.when((side == i) & (t >= 0))
             def _(stream=stream):
@@ -722,11 +755,10 @@
         pl.when((side == 1) & (t + 1 < 36))(lambda: net.grad_piece(t + 1))
         task = turn - 2 - first_task
         pl.when((task >= 0) & (task < 40))(lambda: net.back_task(task))
+        net.sum_vectors(place, turn)
         return carry
 
-    lax.fori_loop(1, 2 * 49 + 2, step, 0)
-    for i in range(4):
-        net.token_copy(i).wait()
+    lax.fori_loop(1, 2 * 48 + 2, step, 0)
 
 
 def greet_all(place):
@@ -746,7 +778,7 @@
 
 
 def whole_layer(*args):
-    anywhere = pl.BlockSpec(memory_space=pl.ANY)
+    anywhere = pl.BlockSpec(memory_space=pltpu.HBM)
     vector = pl.BlockSpec(memory_space=pltpu.VMEM)
     scalars = pl.BlockSpec(memory_space=pltpu.SMEM)
     specs = [anywhere if a.dtype == BF else vector if a.shape[0] >= 768 else scalars for a in args]
@@ -760,56 +792,74 @@
     return pl.pallas_call(
         layer_kernel,
         out_shape=(
-            jax.ShapeDtypeStruct((2,), F32),
-            jax.ShapeDtypeStruct((1024, 768), F32),
-            jax.ShapeDtypeStruct((73 * 128, 768), F32),
+            pltpu.VMEM((8, 128), F32),
+            pltpu.VMEM((1024 + max(1024 + ROWS, 256 * LATE), 768), F32),
+            pltpu.VMEM((16, 768), F32),
+            jax.ShapeDtypeStruct((256 * (36 - LATE), 768), F32),
         ),
         in_specs=specs,
-        out_specs=(scalars, anywhere, anywhere),
+        out_specs=(vector, vector, vector, pl.BlockSpec(memory_space=pltpu.HBM)),
         scratch_shapes=[
             low(N_ACTS, 1024, 768),
             low(768, 768), low(768, 768), low(768, 768), low(768, 768), low(768, 3072), low(3072, 768),
             full(2, 8, 512), full(2, 512, 128), full(2, 512, 128), full(2, 16, 512),
-            full(1024, 768), full(1024, 128), full(1024, 768), full(1024, 128), full(ROWS, 768), full(2, 8, 768),
-            full(2, 16, 16, 128), full(2, 8, 768), full(16, 768), full(2, 256, 768),
+            full(1024, 128), full(1024, 128), full(2, 8, 768),
+            full(2, 16, 16, 128), full(2, 8, 768), full(5, 8, 768), full(2, 256, 768),
             pltpu.SemaphoreType.DMA((7,)), pltpu.SemaphoreType.DMA((16,)), pltpu.SemaphoreType.DMA((16,)),
-            pltpu.SemaphoreType.DMA((4,)),
+            pltpu.SemaphoreType.DMA((6,)), pltpu.SemaphoreType.DMA((6,)),
         ] + stream_scratch() + stream_scratch(),
         compiler_params=pltpu.CompilerParams(
-            collective_id=0, has_side_effects=True, vmem_limit_bytes=63 << 20),
+            collective_id=0, has_side_effects=True, vmem_limit_bytes=VMEM_LIMIT),
     )(*args)
 
 
-def deliver_kernel(count, height, summed, tokens_sum, scores, *refs):
+def deliver_kernel(count, height, summed, late, small, scores, *refs):
     (scores_out, tokens_out, w_q, query_bias, w_k, w_v, value_bias, w_m, mixer_bias, first_gain, first_shift, w_e,
      expand_bias, w_s, shrink_bias, second_gain, second_shift) = refs[:17]
-    buffer, small, came, left, small_came = refs[17:]
+    buffer, came, left, sent = refs[17:]
+
+    def place(row, size):
+        block, at = row // 768, row % 768
+        if block < 4:
+            return w_s.at[pl.ds(row, size)]
+        if block < 8:
+            return w_e.at[pl.ds(at, size), pl.ds(768 * (block - 4), 768)]
+        return (w_m, w_q, w_k, w_v)[block - 8].at[pl.ds(at, size)]
+
+    early = summed.shape[0]
+    direct = [pltpu.make_async_copy(late.at[pl.ds(0, 1024)], tokens_out, sent.at[0])]
+    row = early
+    while row < 9216:
+        size = min(768 - row % 768, 9216 - row)
+        direct.append(pltpu.make_async_copy(
+            late.at[pl.ds(1024 + row - early, size)], place(row, size), sent.at[len(direct)]))
+        row += size
     jobs = []
-    for row in range(0, 3072, height):
-        jobs.append((summed.at[pl.ds(row, height)], w_s.at[pl.ds(row, height)]))
-    for row in range(0, 3072, height):
-        block, at = row // 768, row % 768
-        jobs.append((summed.at[pl.ds(3072 + row, height)], w_e.at[pl.ds(at, height), pl.ds(768 * block, 768)]))
-    for row in range(0, 3072, height):
-        block, at = row // 768, row % 768
-        jobs.append((summed.at[pl.ds(6144 + row, height)], (w_m, w_q, w_k, w_v)[block].at[pl.ds(at, height)]))
-    rows = tokens_sum.shape[0]
-    for row in range(0, rows, height):
-        size = min(height, rows - row)
-        jobs.append((tokens_sum.at[pl.ds(row, size)], tokens_out.at[pl.ds(row, size)]))
+    row = 0
+    while row < early:
+        size = min(height, 768 - row % 768, early - row)
+        jobs.append((row, size))
+        row += size
 
     def copies(i):
-        src, dst = jobs[i]
-        spot = buffer.at[i % count, pl.ds(0, src.shape[0])]
-        return (pltpu.make_async_copy(src, spot, came.at[i % count]),
-                pltpu.make_async_copy(spot, dst, left.at[i % count]))
+        row, size = jobs[i]
+        spot = buffer.at[i % count, pl.ds(0, size)]
+        return (pltpu.make_async_copy(summed.at[pl.ds(row, size)], spot, came.at[i % count]),
+                pltpu.make_async_copy(spot, place(row, size), left.at[i % count]))
 
     total = len(jobs)
     ahead = count // 2
-    vectors = pltpu.make_async_copy(summed.at[pl.ds(9216, 16)], small, small_came)
-    vectors.start()
     for i in range(min(ahead, total)):
         copies(i)[0].start()
+    for copy in direct:
+        copy.start()
+    for j, ref in enumerate((query_bias, value_bias, mixer_bias, first_gain, first_shift, shrink_bias,
+                             second_gain, second_shift)):
+        ref[...] = small[j, :]
+    for j in range(4):
+        expand_bias[768 * j:768 * j + 768] = small[8 + j, :]
+    for s in range(2):
+        scores_out[s] = jnp.sum(scores[s:s + 1, 0:1])
     for i in range(total):
         copies(i)[0].wait()
         copies(i)[1].start()
@@ -818,37 +868,30 @@
             if later >= count:
                 copies(later - count)[1].wait()
             copies(later)[0].start()
-        if i == 0:
-            vectors.wait()
-            for j, ref in enumerate((query_bias, value_bias, mixer_bias, first_gain, first_shift, shrink_bias,
-                                     second_gain, second_shift)):
-                ref[...] = small[j, :]
-            for j in range(4):
-                expand_bias[768 * j:768 * j + 768] = small[8 + j, :]
-            for s in range(2):
-                scores_out[s] = scores[s]
     for i in range(max(0, total - count), total):
         copies(i)[1].wait()
+    for copy in direct:
+        copy.wait()
 
 
 def fused(*args):
-    pair_scores, tokens_grad, summed = whole_layer(*args)
-    anywhere = pl.BlockSpec(memory_space=pl.ANY)
+    pair_scores, late, small, summed = whole_layer(*args)
+    hbm = pl.BlockSpec(memory_space=pltpu.HBM)
     vector = pl.BlockSpec(memory_space=pltpu.VMEM)
     scalars = pl.BlockSpec(memory_space=pltpu.SMEM)
     shapes = [(2,), (1024, 768), (768, 768), (768,), (768, 768), (768, 768), (768,), (768, 768), (768,), (768,), (768,),
               (768, 3072), (3072,), (3072, 768), (768,), (768,), (768,)]
-    count, height = 16, 384
+    count, height = 14, 384
     return tuple(pl.pallas_call(
         partial(deliver_kernel, count, height),
         out_shape=[jax.ShapeDtypeStruct(shape, F32) for shape in shapes],
-        in_specs=[anywhere, pl.BlockSpec(memory_space=pltpu.HBM), scalars],
-        out_specs=[anywhere if len(shape) == 2 else vector if shape[0] > 2 else scalars for shape in shapes],
-        scratch_shapes=[pltpu.VMEM((count, height, 768), F32), pltpu.VMEM((16, 768), F32),
+        in_specs=[hbm, vector, vector, vector],
+        out_specs=[hbm if len(shape) == 2 else vector if shape[0] > 2 else scalars for shape in shapes],
+        scratch_shapes=[pltpu.VMEM((count, height, 768), F32),
                         pltpu.SemaphoreType.DMA((count,)), pltpu.SemaphoreType.DMA((count,)),
-                        pltpu.SemaphoreType.DMA],
-        compiler_params=pltpu.CompilerParams(vmem_limit_bytes=60 << 20),
-    )(summed, tokens_grad, pair_scores))
+                        pltpu.SemaphoreType.DMA((16,))],
+        compiler_params=pltpu.CompilerParams(vmem_limit_bytes=36 << 20),
+    )(summed, late, small, pair_scores))
 
 
 def to_low(value):

time: 286 us -> 280 us (0.979)
  Pallas kernels: 285 us -> 279 us
    pallas_call x1, Pallas kernels: 22.9 us -> 19.2 us  [fused(): pl.pallas_call(partial(deliver_kernel, count, height), out_shape=[jax.Sha...]
where the time goes in v4:
time: 280 us
  Pallas kernels  279 us (100%)
    pallas_call x1, Pallas kernels, whole_layer(): pl.pallas_call(layer_kernel, out_shape=(pltpu.VMEM((8, 128), F32), pltpu....  260 us
    pallas_call x1, Pallas kernels, fused(): pl.pallas_call(partial(deliver_kernel, count, height), out_shape=[jax.Sha...  19.2 us

profile of v4, /device:TPU:0, one launch (start us, length us, event | category | flops | bytes accessed | tf_op | source)
XLA Modules:
  0.0 279.8 jit_solution(13995103437335649965)
XLA Ops:
  0.7 259.8 %shard_map.314 = (f32[8,128]{1,0:T(8,128)S(1)}, f32[3072,768]{1,0:T(8,128)S(1)}, f32[16,768]{1,0:T(8,128)S(1)}, f32[7168,768]{1,0:T(8,128)}) custom-call(bf16[1024,768]{1,0:T(8,128)(2,1)} %refs_0_.1, s32[2]{0:T(128)} %refs_1_.1, s32[64]{0:T(128)} %refs_2_.1, f32[2]{0:T(128)} %refs_3_.1, bf16[768,768]{1,0:T(8,128)(2,1)} %refs_4_.1, f32[768]{0:T(1024)} %refs_5_.1, ...), custom_call_target="tpu_custom_call" | custom-call | tf_op jit(solution)/shard_map/pallas_call | solution.py:792
  260.4 19.2 %shard_map.315 = (f32[2]{0:T(128)}, f32[1024,768]{1,0:T(8,128)}, f32[768,768]{1,0:T(8,128)}, f32[768]{0:T(1024)}, f32[768,768]{1,0:T(8,128)}, /*index=5*/f32[768...) custom-call(f32[7168,768]{1,0:T(8,128)} %get-tuple-element.21.summed, ...), custom_call_target="tpu_custom_call" | custom-call | tf_op jit(solution)/shard_map/pallas_call | solution.py:885

commit v5 on v4

--- a/solution.py
+++ b/solution.py
@@ -50,10 +50,10 @@
         pltpu.VMEM((2, 144, 128), F32),
         pltpu.VMEM((144, 128), F32),
         pltpu.VMEM((2, 144, 128), F32),
-        pltpu.VMEM((72, 128), F32),
-        pltpu.VMEM((2, 72, 128), F32),
-        pltpu.VMEM((72, 128), F32),
-        pltpu.VMEM((2, 72, 128), F32),
+        pltpu.VMEM((80, 128), F32),
+        pltpu.VMEM((2, 80, 128), F32),
+        pltpu.VMEM((64, 128), F32),
+        pltpu.VMEM((2, 64, 128), F32),
         pltpu.VMEM((2, 192, 128), F32),
         pltpu.VMEM((2, 2, 192, 128), F32),
         pltpu.VMEM((128, 128), F32),
@@ -61,7 +61,7 @@
         pltpu.VMEM((4, 64, 128), F32),
         pltpu.VMEM((4, 128, 128), F32),
         pltpu.VMEM((16, 128), F32),
-        pltpu.VMEM((8, 128), F32),
+        pltpu.VMEM((16, 128), F32),
         pltpu.VMEM((8, 64, 768), F32),
         pltpu.SemaphoreType.DMA((10, 2)),
         pltpu.SemaphoreType.DMA((10, 2)),
@@ -107,15 +107,15 @@
 
         slot, row = self.grad_rows(t)
         other = rows_at(row + 64 * (1 - place.c), 64)
-        m = t - 11
-        ring = lax.rem(t + 5, 8)
+        m = t - 10
+        ring = lax.rem(t + 6, 8)
         outs = self.outs(m, 64 * place.c)
         lead = (place.z, 3 - place.z)
         zs = []
         for side, device in ((0, place.up), (1, place.down)):
-            for half, when in ((0, (t >= 1) & (t < n + 5)), (1, (t >= 6) & (t < n + 10))):
+            for half, when in ((0, (t >= 1) & (t < n + 6)), (1, (t >= 7) & (t < n + 9))):
                 for k in range(3):
-                    at, size = (0, 144 - 48 * k) if half == 0 else (144 - 48 * k, 48 + 48 * k)
+                    at, size = (0, 160 - 32 * k) if half == 0 else (160 - 32 * k, 32 + 32 * k)
                     spot = pl.ds(at, size)
                     copy = remote(5 + 2 * side + half, self.z_out.at[side, spot], self.z_in.at[side, par, spot], device)
                     zs.append((copy, when, lead[side] == k, lead[side] == k + 1))
@@ -123,16 +123,14 @@
             (remote(0, self.grad_ref.at[slot, other], self.sib_in.at[par], place.sibling), (t >= 0) & (t < n), True, True),
             (remote(1, self.a_rs_out, self.a_rs_in.at[par], self.to_a), (t >= 1) & (t < n + 1), True, True),
             (tail(1, self.a_rs_out, self.a_rs_in, 128, 16, self.to_a), (t >= n + 1) & (t < n + 4), True, True),
-            (tail(2, self.a_ag_out, self.a_ag_in, 128, 16, self.to_a), (t >= 7) & (t < 10), True, True),
-            (remote(2, self.a_ag_out, self.a_ag_in.at[par], self.to_a), (t >= 10) & (t < n + 10), True, True),
+            (remote(2, self.a_ag_out, self.a_ag_in.at[par], self.to_a), (t >= 6) & (t < n + 7), True, True),
             (remote(3, self.b_rs_out, self.b_rs_in.at[par], self.to_b), (t >= 2) & (t < n + 2), True, True),
-            (tail(3, self.b_rs_out, self.b_rs_in, 64, 8, self.to_b), (t >= n + 2) & (t < n + 5), True, True),
-            (tail(4, self.b_ag_out, self.b_ag_in, 64, 8, self.to_b), (t >= 6) & (t < 9), True, True),
-            (remote(4, self.b_ag_out, self.b_ag_in.at[par], self.to_b), (t >= 9) & (t < n + 9), True, True),
+            (tail(3, self.b_rs_out, self.b_rs_in, 64, 16, self.to_b), (t >= n + 2) & (t < n + 5), True, True),
+            (remote(4, self.b_ag_out, self.b_ag_in.at[par], self.to_b), (t >= 6) & (t < n + 6), True, True),
         ] + zs + [
-            (remote(9, self.full.at[ring], spot, place.sibling), (t >= 11) & (t < n + 11) & when, True, True)
+            (remote(9, self.full.at[ring], spot, place.sibling), (t >= 10) & (t < n + 10) & when, True, True)
             for spot, when in outs
-        ], [(pltpu.make_async_copy(self.full.at[ring], spot, self.kept.at[par]), (t >= 11) & (t < n + 11) & when)
+        ], [(pltpu.make_async_copy(self.full.at[ring], spot, self.kept.at[par]), (t >= 10) & (t < n + 10) & when)
             for spot, when in outs]
 
     def start(self, t):
@@ -175,145 +173,133 @@
         def ring8(stage):
             return lax.rem(t + 16 - stage, 8)
 
-        def got_p(side, pos):
-            return z_in[side, par, 48 * pos:48 * pos + 16, :]
+        def got_p(side):
+            return z_in[side, par, 0:64, :]
 
         def got_q(side, pos, panel):
-            at = 48 * pos + 16 + 16 * panel
+            at = 64 + 32 * pos + 16 * panel
             return z_in[side, par, at:at + 16, :]
 
-        def put_p(side, pos, value):
-            z_out[side, 48 * pos:48 * pos + 16, :] = value
+        def put_p(side, value):
+            z_out[side, 0:64, :] = value
 
         def put_q(side, pos, panel, value):
-            at = 48 * pos + 16 + 16 * panel
+            at = 64 + 32 * pos + 16 * panel
             z_out[side, at:at + 16, :] = value
 
-        def full_p(ring, block, value):
-            self.full[ring, rows16(block), lanes_at((2 * d1 + d2) * 128, 128)] = value
+        def full_p(ring, value):
+            self.full[ring, :, lanes_at((2 * d1 + d2) * 128, 128)] = value
 
         def full_q(ring, block, panel, value):
             self.full[ring, rows16(block), 512 + 128 * panel:640 + 128 * panel] = value
 
-        @pl.when((t >= 11) & (t < self.count + 11))
-        def _stage11():
-            ring = ring8(11)
-            self.full[ring, :, lanes_at((1 - d1) * 256, 128)] = self.a_ag_in[par, 0:64, :]
-            self.full[ring, :, lanes_at((1 - d1) * 256 + 128, 128)] = self.a_ag_in[par, 64:128, :]
+        def live(stage):
+            return (t >= stage) & (t < self.count + stage)
+
+        @pl.when(live(10))
+        def _stage10():
+            ring = ring8(10)
             for side in range(2):
                 @pl.when(lead[side] == 3)
-                def _(side=side, ring=ring):
+                def _(side=side):
                     for panel in range(2):
                         full_q(ring, far(side, 3), panel, got_q(side, 1, panel))
 
-        @pl.when((t >= 10) & (t < self.count + 10))
-        def _stage10():
-            ring = ring8(10)
-            other = self.b_ag_in[par, 0:64, :]
-            self.full[ring, :, lanes_at((2 * d1 + 1 - d2) * 128, 128)] = other
-            self.a_ag_out[rows_at(64 * (1 - d2), 64), :] = other
-            self.a_ag_out[rows_at(64 * d2, 64), :] = self.full[ring, :, lanes_at((2 * d1 + d2) * 128, 128)]
+        @pl.when(live(9))
+        def _stage9():
+            ring = ring8(9)
             for side in range(2):
                 @pl.when(lead[side] >= 2)
-                def _(side=side, ring=ring):
+                def _(side=side):
                     for panel in range(2):
                         value = got_q(side, 2, panel)
                         full_q(ring, far(side, 2), panel, value)
                         put_q(side, 1, panel, value)
 
-        @pl.when((t >= 9) & (t < self.count + 9))
-        def _stage9():
-            ring = ring8(9)
+        @pl.when(live(8))
+        def _stage8():
+            ring = ring8(8)
+            self.full[ring, :, lanes_at((1 - d1) * 256, 128)] = self.a_ag_in[par, 0:64, :]
+            self.full[ring, :, lanes_at((1 - d1) * 256 + 128, 128)] = self.a_ag_in[par, 64:128, :]
             for side in range(2):
-                @pl.when(lead[side] == 3)
-                def _(side=side, ring=ring):
-                    full_p(ring, far(side, 3), got_p(side, 1))
-
                 @pl.when(lead[side] >= 1)
-                def _(side=side, ring=ring):
+                def _(side=side):
                     for panel in range(2):
                         value = got_q(side, 3, panel)
                         full_q(ring, far(side, 1), panel, value)
                         put_q(side, 2, panel, value)
-            self.b_ag_out[0:64, :] = self.full[ring, :, lanes_at((2 * d1 + d2) * 128, 128)]
-
-        @pl.when((t >= 8) & (t < self.count + 8))
-        def _stage8():
-            ring = ring8(8)
-            for side in range(2):
-                @pl.when(lead[side] >= 2)
-                def _(side=side, ring=ring):
-                    value = got_p(side, 2)
-                    full_p(ring, far(side, 2), value)
-                    put_p(side, 1, value)
+
+        @pl.when(live(7))
+        def _stage7():
+            ring = ring8(7)
+            other = self.b_ag_in[par]
+            self.full[ring, :, lanes_at((2 * d1 + 1 - d2) * 128, 128)] = other
+            self.a_ag_out[rows_at(64 * (1 - d2), 64), :] = other
+            self.a_ag_out[rows_at(64 * d2, 64), :] = self.full[ring, :, lanes_at((2 * d1 + d2) * 128, 128)]
             self.full[ring, rows16(z), lanes_at(512 + 128 * (1 - d1), 128)] = self.a_ag_in[par, 128:144, :]
             for panel in range(2):
                 value = self.full[ring, rows16(z), 512 + 128 * panel:640 + 128 * panel]
                 for side in range(2):
                     put_q(side, 3, panel, value)
 
-        @pl.when((t >= 7) & (t < self.count + 7))
-        def _stage7():
-            ring = ring8(7)
-            for side in range(2):
-                @pl.when(lead[side] >= 1)
-                def _(side=side, ring=ring):
-                    value = got_p(side, 3)
-                    full_p(ring, far(side, 1), value)
-                    put_p(side, 2, value)
-            self.full[ring, rows_at(16 * z + 8 * (1 - d2), 8), lanes_at(512 + 128 * d1, 128)] = self.b_ag_in[par, 64:72, :]
-            self.a_ag_out[128:144, :] = self.full[ring, rows16(z), lanes_at(512 + 128 * d1, 128)]
-
-        @pl.when((t >= 6) & (t < self.count + 6))
+        @pl.when(live(6))
         def _stage6():
             ring = ring8(6)
-            value = self.p3[ring4(6), rows16(z), :] + got_p(0, 0) + got_p(1, 0)
-            full_p(ring, z, value)
-            put_p(0, 3, value)
-            put_p(1, 3, value)
-            value = self.q3[...] + self.b_rs_in[par, 64:72, :]
-            self.full[ring, rows_at(16 * z + 8 * d2, 8), lanes_at(512 + 128 * d1, 128)] = value
-            self.b_ag_out[64:72, :] = value
-
-        @pl.when((t >= 5) & (t < self.count + 5))
+            for side in range(2):
+                @pl.when(lead[side] == 3)
+                def _(side=side):
+                    full_p(ring, got_p(side))
+            self.b_ag_out[...] = self.full[ring, :, lanes_at((2 * d1 + d2) * 128, 128)]
+            value = self.q3[...] + self.b_rs_in[par, 64:80, :]
+            self.full[ring, rows16(z), lanes_at(512 + 128 * d1, 128)] = value
+            self.a_ag_out[128:144, :] = value
+
+        @pl.when(live(5))
         def _stage5():
+            ring = ring8(5)
             for side in range(2):
-                @pl.when(lead[side] <= 2)
+                @pl.when(lead[side] == 2)
                 def _(side=side):
-                    put_p(side, 0, self.p3[ring4(5), rows16(target(side, 3)), :] + got_p(side, 1))
-            self.q3[...] = self.q2[rows_at(8 * d2, 8), :] + self.a_rs_in[par, rows_at(128 + 8 * d2, 8), :]
-            self.b_rs_out[64:72, :] = self.q2[rows_at(8 * (1 - d2), 8), :] + self.a_rs_in[par, rows_at(128 + 8 * (1 - d2), 8), :]
-
-        @pl.when((t >= 4) & (t < self.count + 4))
+                    value = self.p3[ring4(5)] + got_p(side)
+                    full_p(ring, value)
+                    put_p(side, value)
+            value = self.q2[...] + self.a_rs_in[par, 128:144, :]
+            self.q3[...] = value
+            self.b_rs_out[64:80, :] = value
+
+        @pl.when(live(4))
         def _stage4():
+            ring = ring4(4)
             for side in range(2):
-                @pl.when(lead[side] <= 1)
+                @pl.when(lead[side] == 1)
                 def _(side=side):
-                    put_p(side, 1, self.p3[ring4(4), rows16(target(side, 2)), :] + got_p(side, 2))
-            ring = ring4(4)
+                    value = self.p3[ring] + got_p(side)
+                    self.p3[ring] = value
+                    put_p(side, value)
 
             def own_q(panel):
                 first = self.q1[ring, rows_at(64 * panel + 16 * z, 16), :]
-                spot = rows_at(16 + 16 * panel, 16)
+                spot = rows_at(64 + 16 * panel, 16)
                 return first + z_in[0, par, spot, :] + z_in[1, par, spot, :]
 
             self.q2[...] = own_q(d1)
             self.a_rs_out[128:144, :] = own_q(1 - d1)
 
-        @pl.when((t >= 3) & (t < self.count + 3))
+        @pl.when(live(3))
         def _stage3():
+            ring = ring4(3)
             for side in range(2):
                 @pl.when(lead[side] <= 2)
                 def _(side=side):
                     for panel in range(2):
-                        own = self.q1[ring4(3), rows_at(64 * panel + 16 * target(side, 3), 16), :]
+                        own = self.q1[ring, rows_at(64 * panel + 16 * target(side, 3), 16), :]
                         put_q(side, 0, panel, own + got_q(side, 1, panel))
-            ring = ring4(3)
-            self.p3[ring] = self.p2[...] + self.b_rs_in[par, 0:64, :]
+            value = self.p2[...] + self.b_rs_in[par, 0:64, :]
+            self.p3[ring] = value
             for side in range(2):
                 @pl.when(lead[side] == 0)
-                def _(side=side, ring=ring):
-                    put_p(side, 2, self.p3[ring, rows16(target(side, 1)), :])
+                def _(side=side):
+                    put_p(side, value)
 
         @pl.when((t >= 2) & (t < self.count + 2))
         def _stage2():
@@ -529,21 +515,22 @@
         share.wait_send()
         share.wait_recv()
 
-    def pair(self, place, s):
-        here = place.me * 2 + s
-        wanted = jnp.full((8, 128), self.partners[here], jnp.int32)
-        mine = self.every[place.c, place.me // 2, 8 * s:8 * s + 8, :]
+    def partners_of(self, place):
+        first = place.me * 2
+        wanted = [jnp.full((8, 128), self.partners[first + s], jnp.int32) for s in range(2)]
 
         def pick(i, found):
-            far, near = found
             device = i // 2
             tile = self.every[lax.rem(device, 2), device // 2, rows_at(8 * lax.rem(i, 2), 8), :]
-            far += jnp.where(wanted == i, tile, 0.0)
-            near += jnp.where(jnp.full((8, 128), self.partners[i], jnp.int32) == here, tile, 0.0)
-            return far, near
-
-        nothing = jnp.zeros((8, 128), F32)
-        far, near = lax.fori_loop(0, 64, pick, (nothing, nothing), unroll=8)
+            chosen = jnp.full((8, 128), self.partners[i], jnp.int32)
+            return tuple(
+                old + jnp.where(hit, tile, 0.0)
+                for old, hit in zip(found, (wanted[0] == i, chosen == first, wanted[1] == i, chosen == first + 1)))
+
+        return lax.fori_loop(0, 64, pick, (jnp.zeros((8, 128), F32),) * 4, unroll=8)
+
+    def pair(self, place, s, far, near):
+        mine = self.every[place.c, place.me // 2, 8 * s:8 * s + 8, :]
         live = lax.broadcasted_iota(jnp.int32, (8, 128), 0) < 6
 
         def inner(left, right):
@@ -734,8 +721,9 @@
     each(1024 // ROWS, net.feed)
     await_all()
     net.gather(place)
+    tiles = net.partners_of(place)
     for s in range(2):
-        net.pair(place, s)
+        net.pair(place, s, tiles[2 * s], tiles[2 * s + 1])
     net.second_vectors()
     each(4, net.back_second)
 
@@ -758,7 +746,7 @@
         net.sum_vectors(place, turn)
         return carry
 
-    lax.fori_loop(1, 2 * 48 + 2, step, 0)
+    lax.fori_loop(1, 2 * 47 + 2, step, 0)
 
 
 def greet_all(place):

time: 280 us -> 278 us (level)
  no operation moved by 1% of the time
where the time goes in v5:
time: 278 us
  Pallas kernels  277 us (100%)
    pallas_call x1, Pallas kernels, whole_layer(): pl.pallas_call(layer_kernel, out_shape=(pltpu.VMEM((8, 128), F32), pltpu....  258 us
    pallas_call x1, Pallas kernels, fused(): pl.pallas_call(partial(deliver_kernel, count, height), out_shape=[jax.Sha...  19.2 us

profile of v5, /device:TPU:0, one launch (start us, length us, event | category | flops | bytes accessed | tf_op | source)
XLA Modules:
  0.0 278.0 jit_solution(4003287388783732842)
XLA Ops:
  0.7 258.0 %shard_map.314 = (f32[8,128]{1,0:T(8,128)S(1)}, f32[3072,768]{1,0:T(8,128)S(1)}, f32[16,768]{1,0:T(8,128)S(1)}, f32[7168,768]{1,0:T(8,128)}) custom-call(bf16[1024,768]{1,0:T(8,128)(2,1)} %refs_0_.1, s32[2]{0:T(128)} %refs_1_.1, s32[64]{0:T(128)} %refs_2_.1, f32[2]{0:T(128)} %refs_3_.1, bf16[768,768]{1,0:T(8,128)(2,1)} %refs_4_.1, f32[768]{0:T(1024)} %refs_5_.1, ...), custom_call_target="tpu_custom_call" | custom-call | tf_op jit(solution)/shard_map/pallas_call | solution.py:780
  258.6 19.2 %shard_map.315 = (f32[2]{0:T(128)}, f32[1024,768]{1,0:T(8,128)}, f32[768,768]{1,0:T(8,128)}, f32[768]{0:T(1024)}, f32[768,768]{1,0:T(8,128)}, /*index=5*/f32[768...) custom-call(f32[7168,768]{1,0:T(8,128)} %get-tuple-element.21.summed, ...), custom_call_target="tpu_custom_call" | custom-call | tf_op jit(solution)/shard_map/pallas_call | solution.py:873

commit v6 on v5

--- a/solution.py
+++ b/solution.py
@@ -487,31 +487,35 @@
         for s in range(2):
             self.logs_t[s] = jnp.transpose(self.logs[s] + jnp.log(self.sums[s]))[0:16, :]
 
+    ORDER = (12, 4, 13, 11, 3, 5, 14, 10, 2, 6, 15, 9, 1, 7, 8)
+
+    def tell_copy(self, place, s, source, device):
+        spot = self.every.at[place.c, source, pl.ds(8 * s, 8)]
+        return pltpu.make_async_remote_copy(
+            src_ref=spot, dst_ref=spot, send_sem=self.told.at[s, device // 2], recv_sem=self.heard.at[s, source],
+            device_id=(device,), device_id_type=MESH)
+
+    def tell(self, place, s):
+        c, chip = place.c, place.me // 2
+        u = self.pool(s)
+        for j in range(6):
+            self.every[c, chip, 8 * s + j:8 * s + j + 1, :] = u[:, 128 * j:128 * j + 128]
+        self.every[c, chip, 8 * s + 6:8 * s + 8, :] = jnp.full((2, 128), self.targets[s], F32)
+        for k in self.ORDER:
+            self.tell_copy(place, s, chip, lax.rem(chip + k, 16) * 2 + c).start()
+
     def gather(self, place):
         c, chip = place.c, place.me // 2
-        every = self.every
         for s in range(2):
-            u = self.pool(s)
-            for j in range(6):
-                every[c, chip, 8 * s + j:8 * s + j + 1, :] = u[:, 128 * j:128 * j + 128]
-            every[c, chip, 8 * s + 6:8 * s + 8, :] = jnp.full((2, 128), self.targets[s], F32)
-
-        def copy(source, device):
-            return pltpu.make_async_remote_copy(
-                src_ref=every.at[c, source], dst_ref=every.at[c, source], send_sem=self.told.at[device // 2],
-                recv_sem=self.heard.at[source], device_id=(device,), device_id_type=MESH)
-
-        order = (12, 4, 13, 11, 3, 5, 14, 10, 2, 6, 15, 9, 1, 7, 8)
-        for k in order:
-            copy(chip, lax.rem(chip + k, 16) * 2 + c).start()
-        for k in order:
-            copy(lax.rem(chip + 16 - k, 16), place.me).wait_recv()
+            for k in self.ORDER:
+                self.tell_copy(place, s, lax.rem(chip + 16 - k, 16), place.me).wait_recv()
         share = pltpu.make_async_remote_copy(
-            src_ref=every.at[c], dst_ref=every.at[c], send_sem=self.told.at[chip],
-            recv_sem=self.heard.at[chip], device_id=(place.sibling,), device_id_type=MESH)
+            src_ref=self.every.at[c], dst_ref=self.every.at[c], send_sem=self.told.at[0, chip],
+            recv_sem=self.heard.at[0, chip], device_id=(place.sibling,), device_id_type=MESH)
         share.start()
-        for k in order:
-            copy(chip, lax.rem(chip + k, 16) * 2 + c).wait_send()
+        for s in range(2):
+            for k in self.ORDER:
+                self.tell_copy(place, s, chip, lax.rem(chip + k, 16) * 2 + c).wait_send()
         share.wait_send()
         share.wait_recv()
 
@@ -718,8 +722,14 @@
     net.turn_logs()
     for copy in loads[4:]:
         copy.wait()
-    each(1024 // ROWS, net.feed)
     await_all()
+
+    def feed_and_tell(i):
+        net.feed(i)
+        for s in range(2):
+            pl.when(i == s)(lambda s=s: net.tell(place, s))
+
+    each(1024 // ROWS, feed_and_tell)
     net.gather(place)
     tiles = net.partners_of(place)
     for s in range(2):
@@ -793,7 +803,7 @@
             full(2, 8, 512), full(2, 512, 128), full(2, 512, 128), full(2, 16, 512),
             full(1024, 128), full(1024, 128), full(2, 8, 768),
             full(2, 16, 16, 128), full(2, 8, 768), full(5, 8, 768), full(2, 256, 768),
-            pltpu.SemaphoreType.DMA((7,)), pltpu.SemaphoreType.DMA((16,)), pltpu.SemaphoreType.DMA((16,)),
+            pltpu.SemaphoreType.DMA((7,)), pltpu.SemaphoreType.DMA((2, 16)), pltpu.SemaphoreType.DMA((2, 16)),
             pltpu.SemaphoreType.DMA((6,)), pltpu.SemaphoreType.DMA((6,)),
         ] + stream_scratch() + stream_scratch(),
         compiler_params=pltpu.CompilerParams(

time: 278 us -> 278 us (level)
  no operation moved by 1% of the time
where the time goes in v6:
time: 278 us
  Pallas kernels  277 us (100%)
    pallas_call x1, Pallas kernels, whole_layer(): pl.pallas_call(layer_kernel, out_shape=(pltpu.VMEM((8, 128), F32), pltpu....  258 us
    pallas_call x1, Pallas kernels, fused(): pl.pallas_call(partial(deliver_kernel, count, height), out_shape=[jax.Sha...  19.2 us

profile of v6, /device:TPU:0, one launch (start us, length us, event | category | flops | bytes accessed | tf_op | source)
XLA Modules:
  0.0 278.0 jit_solution(15461644318090923819)
XLA Ops:
  0.7 257.9 %shard_map.314 = (f32[8,128]{1,0:T(8,128)S(1)}, f32[3072,768]{1,0:T(8,128)S(1)}, f32[16,768]{1,0:T(8,128)S(1)}, f32[7168,768]{1,0:T(8,128)}) custom-call(bf16[1024,768]{1,0:T(8,128)(2,1)} %refs_0_.1, s32[2]{0:T(128)} %refs_1_.1, s32[64]{0:T(128)} %refs_2_.1, f32[2]{0:T(128)} %refs_3_.1, bf16[768,768]{1,0:T(8,128)(2,1)} %refs_4_.1, f32[768]{0:T(1024)} %refs_5_.1, ...), custom_call_target="tpu_custom_call" | custom-call | tf_op jit(solution)/shard_map/pallas_call | solution.py:790
  258.6 19.2 %shard_map.315 = (f32[2]{0:T(128)}, f32[1024,768]{1,0:T(8,128)}, f32[768,768]{1,0:T(8,128)}, f32[768]{0:T(1024)}, f32[768,768]{1,0:T(8,128)}, /*index=5*/f32[768...) custom-call(f32[7168,768]{1,0:T(8,128)} %get-tuple-element.21.summed, ...), custom_call_target="tpu_custom_call" | custom-call | tf_op jit(solution)/shard_map/pallas_call | solution.py:883
